TPU v7x, 256 devices: a whole 4x4x8 slice. The times are simulated.
256 devices in a mesh: leaf: 16 (over z, core), probe: 16 (over y, x).
Axes of the slice: x: 4, y: 4, z: 8, core: 2. Of those that a mesh axis runs over, the one named last changes fastest.
Arguments:
- points: bfloat16 [8, 65536], P(None, 'leaf'), may hold values from -6 to 6
- values: bfloat16 [64, 65536], P('probe', 'leaf'), may hold values from -6 to 6
- order: int32 [16, 4096], P('leaf'), may hold values from 0 to 4095, each once within a row
- block_list: int32 [256, 8], P('leaf'), may hold values from 0 to 255, as said below
- leaf_basis: bfloat16 [256, 256, 256], P('leaf'), may hold values from -0.375 to 0.375
- local_transfers: bfloat16 [16, 30, 2, 256, 256], P('leaf'), may hold values from -0.25 to 0.25
- chain_transfers: bfloat16 [16, 4, 2, 256, 256], P('leaf', None, None, 'probe'), as said below
Outputs:
- product: float32 [64, 65536], P('probe', 'leaf')
Inputs may be any that keep to these rules, and one draw needn't show every extreme that they name: `block_list`: row i lists leaf i first, then 8 - 1 leaves j with 1 <= |j - i| <= 16; entries may repeat. `order`: each row is a permutation. `chain_transfers`: slot j of device d holds the pair of the level 4 + j node above d; all devices under one node hold the same pair.
All inputs are finite; a program needn't handle non-finite values.
Results may differ from a plain program's by a relative error of at most 0.0028.
Values may be sent and summed in bfloat16 or wider, within the bound.
No kernel may reach another device: no remote copies, remote signals or barrier semaphores. Data moves between devices by JAX's collectives and lax.ppermute only.
A program may use at most 64 MiB of HBM per device.

v0:
```python
import jax
import jax.numpy as jnp
from jax import lax
from jax.sharding import PartitionSpec as P

PRECISE = lax.Precision.HIGHEST


def padded_2(cells, sides, width):
    for axis, dim in sides:
        count = lax.axis_size(axis)
        ends = count - 1
        head = lax.slice_in_dim(cells, 0, width, axis=dim)
        tail = lax.slice_in_dim(cells, cells.shape[dim] - width, cells.shape[dim], axis=dim)
        cells = jnp.concatenate(
            [
                lax.ppermute(tail, axis, [(i, (i + 1) % count) for i in range(ends)]),
                cells,
                lax.ppermute(head, axis, [((i + 1) % count, i) for i in range(ends)]),
            ],
            axis=dim,
        )
    return cells


def swapped(value, axis, bit):
    mask = 2**bit
    pairs = [(source, source ^ mask) for source in range(lax.axis_size(axis))]
    return lax.ppermute(value, axis, pairs)


def kernel_tile(source, target):
    source = source.astype(jnp.float32)
    target = target.astype(jnp.float32)
    inner_prod = jnp.einsum("dnq,dp->nqp", source, target, precision=PRECISE)
    squared = (
        jnp.sum(source * source, 0)[:, :, None]
        + jnp.sum(target * target, 0)[None, None, :]
        - 2.0 * inner_prod
    )
    factor = 1.0 + squared * 0.125
    return 1.0 / (factor * factor * factor)


def pair_fields(partial_value):
    upward = partial_value[:, 0]
    coupled = partial_value[:, 1]
    node_count = upward.shape[0]
    merged = upward[0::2] + upward[1::2]
    crossed = coupled.reshape(node_count // 2, 2, coupled.shape[1], coupled.shape[2])[
        :, ::-1
    ].reshape(coupled.shape)
    return (merged, crossed)


def lift_terms(matrices, skeleton):
    return jnp.einsum("nmab,nac->nmbc", matrices.astype(jnp.float32), skeleton, precision=PRECISE)


def push_down(matrices, parent):
    return jnp.einsum("nab,nbc->nac", matrices.astype(jnp.float32), parent, precision=PRECISE)


def shards(points, values, order, block_list, leaf_basis, local_transfers, chain_transfers):
    coord_dim = points.shape[0]
    columns = values.shape[0]
    leaf_dev, leaf_size, rank_size = leaf_basis.shape
    chain_depth = lax.axis_size("leaf").bit_length() - 1
    local_levels = leaf_dev.bit_length() - 1
    joined = jnp.take(jnp.concatenate([points, values], 0), order[0], axis=1)
    tree_data = joined.reshape(coord_dim + columns, leaf_dev, leaf_size)
    padded = padded_2(tree_data, (("leaf", 1),), leaf_dev)
    first_leaf = lax.axis_index("leaf") * leaf_dev
    window_slots = block_list - first_leaf + leaf_dev

    def near_leaf(leaf_index):
        own_coords = lax.dynamic_index_in_dim(tree_data, leaf_index, 1, keepdims=False)[:coord_dim]
        picked = jnp.take(padded, window_slots[leaf_index], axis=1)
        near_tile = kernel_tile(picked[:coord_dim], own_coords).astype(jnp.bfloat16)
        return jnp.einsum(
            "cnq,nqp->cp", picked[coord_dim:], near_tile, preferred_element_type=jnp.float32
        )

    near_cols = jnp.swapaxes(lax.map(near_leaf, jnp.arange(leaf_dev, dtype=jnp.int32)), 0, 1)
    skeleton = jnp.einsum(
        "lqr,clq->lrc", leaf_basis, tree_data[coord_dim:], preferred_element_type=jnp.float32
    )
    fields = []
    slot_start = 0
    for tree_level in range(local_levels):
        node_count = leaf_dev >> tree_level
        matrices = local_transfers[0, slot_start : slot_start + node_count]
        skeleton, crossed = pair_fields(lift_terms(matrices, skeleton))
        fields.append(crossed)
        slot_start += node_count
    root_skeleton = skeleton[0]
    chain_fields = []
    rank_part = lax.all_to_all(root_skeleton, "probe", split_axis=0, concat_axis=1, tiled=True)
    for chain_step in range(chain_depth):
        matrices = chain_transfers[0, chain_step]
        partial_value = jnp.einsum(
            "mab,ac->mbc", matrices.astype(jnp.float32), rank_part, precision=PRECISE
        )
        summed = lax.psum_scatter(partial_value, "probe", scatter_dimension=1, tiled=True)
        sibling = swapped(summed, "leaf", chain_step)
        rank_part = summed[0] + sibling[0]
        chain_fields.append(sibling[1])
    node_field = chain_fields[chain_depth - 1]
    full_field = node_field
    for chain_step in range(chain_depth - 2, -2, -1):
        full_field = lax.all_gather(node_field, "probe", axis=0, tiled=True)
        if chain_step >= 0:
            lowered = jnp.dot(
                chain_transfers[0, chain_step, 0].astype(jnp.float32), full_field, precision=PRECISE
            )
            node_field = chain_fields[chain_step] + lowered
    root_field = lax.dynamic_slice_in_dim(full_field, lax.axis_index("probe") * columns, columns, 1)
    node_field = root_field[None]
    slot_start = 2 * leaf_dev - 2
    for tree_level in range(local_levels - 1, -1, -1):
        node_count = leaf_dev >> tree_level
        slot_start -= node_count
        matrices = local_transfers[0, slot_start : slot_start + node_count, 0]
        node_field = fields[tree_level] + push_down(matrices, jnp.repeat(node_field, 2, axis=0))
    far_part = jnp.einsum(
        "lqr,lrc->clq", leaf_basis.astype(jnp.float32), node_field, precision=PRECISE
    )
    combined = near_cols + far_part
    flattened = combined.reshape(columns, leaf_dev * leaf_size)
    return jnp.zeros_like(flattened).at[:, order[0]].set(flattened)


def solution(mesh):
    placed = (
        P(None, "leaf"),
        P("probe", "leaf"),
        P("leaf", None),
        P("leaf", None),
        P("leaf", None, None),
        P("leaf", None, None, None, None),
        P("leaf", None, None, "probe", None),
    )
    return jax.shard_map(
        shards, mesh=mesh, in_specs=placed, out_specs=P("probe", "leaf"), check_vma=False
    )
```

profile of v0, /device:TPU:24, one launch (start us, length us, event | category | flops | bytes accessed | tf_op | source)
XLA Modules:
  0.0 641.4 jit_solution(14776533647374316370)
XLA Ops:
  9.0 1.4 copy.60
  10.4 12.4 %gather_fusion.1 = bf16[4096,12]{1,0:T(8,128)(2,1)S(1)} fusion(bf16[12,4096]{0,1:T(8,128)(2,1)} %copy.60, s32[4096]{0:T(1024)S(1)} %broadcast_clamp_fusion), kind=kCustom, calls=%fused_computation.1 | custom fusion | bytes 212992 | tf_op jit(solution)/shard_map/jit(_take)/gather | solution.py:70
  22.8 2.2 slice_select_fusion
  25.5 3.9 fusion.18
  29.4 2.5 fusion.21
  32.0 1.7 convolution_bitcast_fusion.7
  33.7 1.4 convolution_bitcast_fusion.9
  35.2 12.6 %all_to_all.16 = f32[16,16,4]{1,2,0:T(4,128)S(1)} all-to-all(f32[16,16,4]{1,2,0:T(4,128)S(1)} %copy.64), channel_id=1, replica_groups=mesh['leaf'=16,'probe'=16] {'probe'}, dimensions={0} | all-to-all | bytes 8192 | tf_op jit(solution)/shard_map/all_to_all | solution.py:98
  50.2 93.5 %all-reduce.9.cloned.1.call-done = f32[2,256,64]{2,0,1:T(2,128)} async-done(((f32[2,256,64]{2,0,1:T(2,128)}), f32[2,256,64]{2,0,1:T(2,128)}) %all-reduce.9.cloned.1.call-update) | async-done | bytes 131088
  148.0 93.0 %all-reduce.11.cloned.1.call-done = f32[2,256,64]{2,0,1:T(2,128)} async-done(((f32[2,256,64]{2,0,1:T(2,128)}), f32[2,256,64]{2,0,1:T(2,128)}) %all-reduce.11.cloned.1.call-update) | async-done | bytes 131088
  241.7 1.6 collective-permute-start.3
  243.7 1.9 collective-permute-done.3
  247.5 1.3 collective-permute-start.1
  248.8 3.0 collective-permute-start
  251.8 89.5 %all-reduce.13.cloned.1.call-done = f32[2,256,64]{2,0,1:T(2,128)} async-done(((f32[2,256,64]{2,0,1:T(2,128)}), f32[2,256,64]{2,0,1:T(2,128)}) %all-reduce.13.cloned.1.call-update) | async-done | bytes 131088
  342.0 2.5 collective-permute-start.4
  344.6 2.0 collective-permute-done.4
  347.9 93.8 %all-reduce.15.cloned.1.call-done = f32[2,256,64]{2,0,1:T(2,128)} async-done(((f32[2,256,64]{2,0,1:T(2,128)}), f32[2,256,64]{2,0,1:T(2,128)}) %all-reduce.15.cloned.1.call-update) | async-done | bytes 131088
  442.5 5.7 collective-permute-start.5
  448.2 69.1 %while.10 = (s32[]{:T(128)}, f32[16,4,256]{2,1,0:T(4,128)S(1)}, s32[16]{0:T(128)S(1)}, s32[16,8]{1,0:T(8,128)S(1)}, bf16[12,48,256]{2,0,1:T(8,128)(2,1)S(1)}, /*...) while((s32[]{:T(128)}, f32[16,4,256]{2,1,0:T(4,128)S(1)}, s32[16]{0:T(128)S(1)}, ...), condition=%wide.region_3.4_spmd, body=%wide.region_0.3_spmd.sunk | while | flops 17380172 | bytes 2410839 | solution.py:84
  517.3 21.5 %all-gather = f32[1,256,64]{2,0,1:T(1,128)S(1)} all-gather(f32[1,16,64]{2,0,1:T(1,128)S(1)} %slice.212), channel_id=2, replica_groups=mesh['leaf'=16,'probe'=16] {'probe'}, dimensions={1}, use_global_device_ids=true | all-gather | bytes 69632 | tf_op jit(solution)/shard_map/all_gather | solution.py:111
  539.0 22.9 %all_gather.13 = f32[256,64]{1,0:T(8,128)S(1)} all-gather(f32[16,64]{1,0:T(8,128)S(1)} %fusion.64), channel_id=1, replica_groups=mesh['leaf'=16,'probe'=16] {'probe'}, dimensions={0}, use_global_device_ids=true | all-gather | bytes 69632 | tf_op jit(solution)/shard_map/all_gather | solution.py:111
  562.7 21.5 %all_gather.14 = f32[256,64]{1,0:T(8,128)S(1)} all-gather(f32[16,64]{1,0:T(8,128)S(1)} %fusion.68), channel_id=1, replica_groups=mesh['leaf'=16,'probe'=16] {'probe'}, dimensions={0}, use_global_device_ids=true | all-gather | bytes 69632 | tf_op jit(solution)/shard_map/all_gather | solution.py:111
  584.4 23.1 %all_gather.15 = f32[256,64]{1,0:T(8,128)S(1)} all-gather(f32[16,64]{1,0:T(8,128)S(1)} %fusion.72), channel_id=1, replica_groups=mesh['leaf'=16,'probe'=16] {'probe'}, dimensions={0}, use_global_device_ids=true | all-gather | bytes 69632 | tf_op jit(solution)/shard_map/all_gather | solution.py:111
  607.6 1.3 fusion.32
  608.9 1.6 fusion.31
  610.5 2.1 fusion.30
  612.7 3.3 fusion.27
  616.0 1.7 fusion.90
  617.8 2.0 copy.81
  619.8 12.3 %scatter_custom_fusion = f32[4,4096]{0,1:T(8,128)} fusion(s32[4096]{0:T(1024)S(1)} %bitcast.262, f32[4096,4]{1,0:T(8,128)} %copy.81, f32[]{:T(128)} %constant.37.clone.1), kind=kCustom, calls=%fused_computation.56 | custom fusion | bytes 66048 | tf_op jit(solution)/shard_map/scatter | solution.py:130
  632.1 2.8 copy.82
  (236 shorter events, 54.7 us)
Async XLA Ops:
  6.5 18.5 %copy-start = (bf16[16,256,256]{2,1,0:T(8,128)(2,1)S(1)}, bf16[16,256,256]{2,1,0:T(8,128)(2,1)}, u32[]{:S(2)}) copy-start(bf16[16,256,256]{2,1,0:T(8,128)(2,1)} %param.13) | copy-start | bytes 6291460
  6.5 137.2 %all-reduce.9.cloned.1.call-start = ((), (), s32[]{:S(2)}) async-start(), calls=%async_computation.1 | async-start | bytes 524288
  29.4 18.4 %copy-start.2 = (bf16[1,4,2,16,256]{4,3,2,1,0:T(8,128)(2,1)S(1)}, bf16[1,4,2,16,256]{4,3,2,1,0:T(8,128)(2,1)}, u32[]{:S(2)}) copy-start(bf16[1,4,2,16,256]{4,3,2,1,0:T(8,128)(2,1)} %param.15) | copy-start | bytes 196612
  29.4 19.5 %copy-start.4 = (u32[256]{0:T(256)S(1)}, u32[256]{0:T(256)}, u32[]{:S(2)}) copy-start(u32[256]{0:T(256)} %constant.79) | copy-start | bytes 3076
  32.0 115.3 %copy-start.1 = (s32[1,4096]{1,0:T(1,128)S(1)}, s32[1,4096]{1,0:T(1,128)}, u32[]{:S(2)}) copy-start(s32[1,4096]{1,0:T(1,128)} %param.11) | copy-start | bytes 49156
  47.8 296.7 %copy-start.3 = (s32[16,8]{0,1:T(8,128)S(1)}, s32[16,8]{0,1:T(8,128)}, u32[]{:S(2)}) copy-start(s32[16,8]{0,1:T(8,128)} %param.12) | copy-start | bytes 1540
  48.9 192.1 %all-reduce.11.cloned.1.call-start = ((), (), s32[]{:S(2)}) async-start(), calls=%async_computation.2 | async-start | bytes 524288
  144.4 1.2 collective-permute-start.2
  146.7 194.5 %all-reduce.13.cloned.1.call-start = ((), (), s32[]{:S(2)}) async-start(), calls=%async_computation.3 | async-start | bytes 524288
  241.7 3.8 collective-permute-start.3
  247.4 194.4 %all-reduce.15.cloned.1.call-start = ((), (), s32[]{:S(2)}) async-start(), calls=%async_computation.4 | async-start | bytes 524288
  247.5 100.4 %collective-permute-start.1 = (bf16[12,16,256]{2,0,1:T(8,128)(2,1)S(1)}, bf16[12,16,256]{2,0,1:T(8,128)(2,1)S(1)}, u32[]{:S(2)}, u32[]{:S(2)}) collective-permute-start(bf16[12,16,256]{2,0,1:T(8,128)(2,1)S(1)} %broadcast_select_fusion), channel_id=1, source_target_pairs={{16,0},{32,16},{48,32},{64,48},{80,64},{96,80},{112,96},{128,112},... | collective-permute-start | bytes 294920 | tf_op jit(solution)/shard_map/ppermute | solution.py:19
  248.8 99.1 %collective-permute-start = (bf16[12,16,256]{2,0,1:T(8,128)(2,1)S(1)}, bf16[12,16,256]{2,0,1:T(8,128)(2,1)S(1)}, u32[]{:S(2)}, u32[]{:S(2)}) collective-permute-start(bf16[12,16,256]{2,0,1:T(8,128)(2,1)S(1)} %broadcast_select_fusion), channel_id=1, source_target_pairs={{0,16},{16,32},{32,48},{48,64},{64,80},{80,96},{96,112},{112,128},... | collective-permute-start | bytes 294920 | tf_op jit(solution)/shard_map/ppermute | solution.py:17
  342.0 4.6 collective-permute-start.4
  442.5 74.8 %collective-permute-start.5 = (f32[2,16,64]{2,0,1:T(2,128)S(1)}, f32[2,16,64]{2,0,1:T(2,128)S(1)}, u32[]{:S(2)}, u32[]{:S(2)}) collective-permute-start(f32[2,16,64]{2,0,1:T(2,128)S(1)} %constant_dynamic-slice_fusion.1), channel_id=1, source_target_pairs={{0,128},{16,144},{32,160},{48,176},{64,192},{80,208},{96,224},{112... | collective-permute-start | bytes 24584 | tf_op jit(solution)/shard_map/ppermute | solution.py:29
Sparse Core Ops, SparseCore 0:
  49.0 94.6 all-reduce.8
  147.2 93.7 all-reduce.10
  247.5 93.7 all-reduce.12
  347.9 93.8 all-reduce.14
where the time goes:
time: 644 us; the launch traced here: 641 us
  waiting for transfers between devices  375 us (58%)
  blocking collectives  102 us (16%)
  local copies, waits for them, and re-layouts  57.5 us (9%)
  matrix products  40.4 us (6%)
  loops' own time  30.5 us (5%)
  starting transfers between devices  14.3 us (2%)
  between operations  14.1 us (2%)
  other arithmetic  8.12 us (1%)
    unnamed x8, waiting for transfers between devices  370 us
    all_gather x4, blocking collectives, shards(): full_field = lax.all_gather(node_field, 'probe', axis=0, tiled=True)  89 us
    another operation x1, loops' own time, shards(): lax.map(near_leaf, jnp.arange(leaf_dev, dtype=jnp.int32))  30.5 us
    scatter x2, local copies, waits for them, and re-layouts, shards(): return jnp.zeros_like(flattened).at[:, order[0]].set(flattened)  15.1 us
    dot_general x16, matrix products, kernel_tile(): inner_prod = jnp.einsum('dnq,dp->nqp', source, target, precision=PRECISE)  13.4 us
  transfers between devices with their start and end apart: 10, of which 7 were waited for; matrix products, arithmetic and copies ran while one was open for 7% of the time, Pallas kernels for 0%

commit v1 on v0

v1 whole, which is shorter than its diff:
```python
import functools
import jax
import jax.numpy as jnp
from jax import lax
from jax.experimental import pallas as pl
from jax.experimental.pallas import tpu as pltpu
from jax.sharding import PartitionSpec as P

F32 = jnp.float32
BF = jnp.bfloat16
MB = 2**20
NT = (((1,), (1,)), ((), ()))
NN = (((1,), (0,)), ((), ()))
VM = pl.BlockSpec(memory_space=pltpu.VMEM)
SM = pl.BlockSpec(memory_space=pltpu.SMEM)
ANY = pl.BlockSpec(memory_space=pl.ANY)


def dot(a, b, dims=NN):
    return lax.dot_general(a, b, dims, preferred_element_type=F32)


def split(s):
    hi = s.astype(BF).astype(F32)
    return jnp.concatenate([hi, s - hi], 0).astype(BF)


def dot2(left, mat, dims=NN):
    r = dot(left, mat, dims)
    return r[:8] + r[8:]


def tree_kernel(points, values, order, td, xs, xr):
    xs[0:8, :] = points[...].astype(F32)
    xs[8:16, :] = jnp.zeros((8, xs.shape[1]), F32)
    xs[8:12, :] = values[...].astype(F32)
    for h in range(16):
        xr[h * 16 : h * 16 + 16, :] = xs[:, h * 256 : h * 256 + 256].astype(BF)
    rows = lax.broadcasted_iota(jnp.int32, (256, 256), 0)
    sub = lax.broadcasted_iota(jnp.int32, (8, 256), 0)
    for t in range(16):
        o = order[:, t * 256 : t * 256 + 256]
        oh = jnp.where(rows == (o & 255), 1.0, 0.0).astype(BF)
        z = dot(xr[...], oh)
        hi = o >> 8
        low = jnp.zeros((8, 256), F32)
        high = jnp.zeros((8, 256), F32)
        for h in range(16):
            low = jnp.where(hi == h, z[h * 16 : h * 16 + 8], low)
            high = jnp.where(hi == h, z[h * 16 + 8 : h * 16 + 16], high)
        m = jnp.sum(low * low, 0, keepdims=True) * 0.125
        mh = m.astype(BF).astype(F32)
        high = jnp.where(sub == 4, mh, jnp.where(sub == 5, m - mh, jnp.where(sub >= 6, 1.0, high)))
        td[t] = jnp.concatenate([low, high], 0).astype(BF)


def tree(points, values, order):
    return pl.pallas_call(
        tree_kernel,
        out_shape=jax.ShapeDtypeStruct((16, 16, 256), BF),
        in_specs=[VM] * 3,
        out_specs=VM,
        scratch_shapes=[pltpu.VMEM((16, 4096), F32), pltpu.VMEM((256, 256), BF)],
        compiler_params=pltpu.CompilerParams(vmem_limit_bytes=8 * MB),
        name="tree",
    )(points, values, order)


LEVELS = ((0, 16), (16, 8), (24, 4), (28, 2))


def up_kernel(td, basis, lt, g, root, bas, ltv, s, sem):
    copies = []

    def start(src, dst):
        c = pltpu.make_async_copy(src, dst, sem.at[len(copies)])
        c.start()
        copies.append(c)

    for q in range(2):
        start(basis.at[pl.ds(q * 8, 8)], bas.at[pl.ds(q * 8, 8)])
    for q in range(4):
        start(lt.at[0, pl.ds(q * 4, 4)], ltv.at[pl.ds(q * 4, 4)])
    for q in range(2):
        start(lt.at[0, pl.ds(16 + q * 4, 4)], ltv.at[pl.ds(16 + q * 4, 4)])
    start(lt.at[0, pl.ds(24, 6)], ltv.at[pl.ds(24, 6)])
    sub = lax.broadcasted_iota(jnp.int32, (8, 256), 0)
    for l in range(16):
        if l % 8 == 0:
            copies[l // 8].wait()
        r = dot(td[l], bas[l])
        s[l] = jnp.where(sub < 4, r[8:], 0.0)
    for start_slot, count in LEVELS:
        for n in range(0, count, 2):
            slot = start_slot + n
            if slot % 4 == 0 and slot < 24:
                copies[2 + slot // 4].wait()
            if slot == 24:
                copies[8].wait()
            l0 = split(s[n])
            l1 = split(s[n + 1])
            g[slot + 1] = dot2(l0, ltv[slot, 1])
            g[slot] = dot2(l1, ltv[slot + 1, 1])
            s[n // 2] = dot2(l0, ltv[slot, 0]) + dot2(l1, ltv[slot + 1, 0])
    root[...] = s[0]


def up(td, basis, lt):
    return pl.pallas_call(
        up_kernel,
        out_shape=(jax.ShapeDtypeStruct((30, 8, 256), F32), jax.ShapeDtypeStruct((8, 256), F32)),
        in_specs=[VM, ANY, ANY],
        out_specs=(VM, VM),
        scratch_shapes=[
            pltpu.VMEM((16, 256, 256), BF),
            pltpu.VMEM((30, 2, 256, 256), BF),
            pltpu.VMEM((16, 8, 256), F32),
            pltpu.SemaphoreType.DMA((9,)),
        ],
        compiler_params=pltpu.CompilerParams(vmem_limit_bytes=16 * MB),
        name="up",
    )(td, basis, lt)


def near_kernel(variant, recip, unroll, slots, left, own, right, out, win, tr):
    win[0:16] = left[...]
    win[16:32] = own[...]
    win[32:48] = right[...]
    sub = lax.broadcasted_iota(jnp.int32, (16, 256), 0)

    def pside(l):
        p = own[l].astype(F32)
        m = jnp.sum(jnp.where(sub < 8, p * p, 0.0), 0, keepdims=True) * 0.125 + 1.0
        mh = m.astype(BF).astype(F32)
        return jnp.where(
            sub < 8, p * -0.25,
            jnp.where(sub < 12, 0.0, jnp.where(sub < 14, 1.0, jnp.where(sub == 14, mh, m - mh))))

    def inv(f):
        c = f * f * f
        if recip == "approx":
            return pl.reciprocal(c, approx=True).astype(BF)
        if recip == "newton":
            r = pl.reciprocal(c, approx=True)
            return (r * (2.0 - c * r)).astype(BF)
        return (1.0 / c).astype(BF)

    if variant == "A":
        def leaf(l, carry):
            pt = pside(l).T.astype(BF)
            acc = jnp.zeros((16, 256), F32)
            for n in range(8):
                q = win[slots[l, n]]
                f = dot(pt, q)
                acc = acc + dot(q, inv(f), NT)
            out[l] = acc[8:]
            return carry
    else:
        def tl(l, carry):
            tr[l] = win[l].astype(F32).T.astype(BF)
            return carry
        lax.fori_loop(0, 48, tl, 0, unroll=4)

        def leaf(l, carry):
            pt = pside(l).astype(BF)
            acc = jnp.zeros((16, 256), F32)
            for n in range(8):
                j = slots[l, n]
                f = dot(tr[j], pt)
                acc = acc + dot(win[j], inv(f))
            out[l] = acc[8:]
            return carry

    lax.fori_loop(0, 16, leaf, 0, unroll=unroll)


def near(slots, left, own, right, variant="A", recip="approx", unroll=1):
    return pl.pallas_call(
        functools.partial(near_kernel, variant, recip, unroll),
        out_shape=jax.ShapeDtypeStruct((16, 8, 256), F32),
        in_specs=[SM, VM, VM, VM],
        out_specs=VM,
        scratch_shapes=[pltpu.VMEM((48, 16, 256), BF), pltpu.VMEM((48, 256, 16), BF)],
        compiler_params=pltpu.CompilerParams(vmem_limit_bytes=16 * MB),
        name="near",
    )(slots, left, own, right)


def down_kernel(order, cf, near_f, g, chain, basis, lt, out, bas, ltv, f, cb, sem):
    copies = []

    def start(src, dst):
        c = pltpu.make_async_copy(src, dst, sem.at[len(copies)])
        c.start()
        copies.append(c)

    start(lt.at[0, pl.ds(24, 6), 0], ltv.at[pl.ds(24, 6)])
    start(lt.at[0, pl.ds(16, 8), 0], ltv.at[pl.ds(16, 8)])
    for q in range(2):
        start(lt.at[0, pl.ds(8 * q, 8), 0], ltv.at[pl.ds(8 * q, 8)])
    for q in range(2):
        start(basis.at[pl.ds(q * 8, 8)], bas.at[pl.ds(q * 8, 8)])
    top = cf[3]
    for k in (2, 1, 0):
        top = cf[k] + dot2(split(top), chain[2 * k], NT)
    f[0] = top
    for start_slot, count in LEVELS[::-1]:
        if start_slot == 28:
            copies[0].wait()
        if start_slot == 16:
            copies[1].wait()
        for m in range(count // 2 - 1, -1, -1):
            slot = start_slot + 2 * m
            if start_slot == 0 and m == 7:
                copies[3].wait()
            if start_slot == 0 and m == 3:
                copies[2].wait()
            l = split(f[m])
            f[2 * m + 1] = g[slot + 1] + dot2(l, ltv[slot + 1], NT)
            f[2 * m] = g[slot] + dot2(l, ltv[slot], NT)
    for l in range(16):
        if l % 8 == 0:
            copies[4 + l // 8].wait()
        tot = near_f[l] + dot2(split(f[l]), bas[l], NT)
        cb[:, l * 256 : l * 256 + 256] = tot
    rows = lax.broadcasted_iota(jnp.int32, (256, 256), 0)
    hrow = lax.broadcasted_iota(jnp.int32, (16, 256), 0)
    acc = jnp.zeros((128, 256), F32)
    for t in range(16):
        o = order[:, t * 256 : t * 256 + 256]
        oh = jnp.where(rows == (o & 255), 1.0, 0.0).astype(BF)
        hit = hrow == (o >> 8)
        c = cb[:, t * 256 : t * 256 + 256]
        ch = c.astype(BF).astype(F32)
        cl = c - ch
        parts = [jnp.where(hit, part[k : k + 1], 0.0) for k in range(4) for part in (ch, cl)]
        acc = acc + dot(jnp.concatenate(parts, 0).astype(BF), oh, NT)
    for k in range(4):
        both = acc[k * 32 : k * 32 + 16] + acc[k * 32 + 16 : k * 32 + 32]
        for h in range(16):
            out[k : k + 1, h * 256 : h * 256 + 256] = both[h : h + 1]


def down(order, cf, near_f, g, chain, basis, lt):
    return pl.pallas_call(
        down_kernel,
        out_shape=jax.ShapeDtypeStruct((4, 4096), F32),
        in_specs=[VM] * 5 + [ANY] * 2,
        out_specs=VM,
        scratch_shapes=[
            pltpu.VMEM((16, 256, 256), BF),
            pltpu.VMEM((30, 256, 256), BF),
            pltpu.VMEM((16, 8, 256), F32),
            pltpu.VMEM((8, 4096), F32),
            pltpu.SemaphoreType.DMA((6,)),
        ],
        compiler_params=pltpu.CompilerParams(vmem_limit_bytes=16 * MB),
        name="down",
    )(order, cf, near_f, g, chain, basis, lt)


def chain_kernel(*refs):
    root, groups, c, w, = refs[0], refs[1:5], refs[5], refs[6]
    me = lax.axis_index("probe")
    y, x = me // 4, lax.rem(me, 4)
    for ky in range(4):
        for kx in range(4):
            src = lax.rem(y + 4 - ky, 4) * 4 + lax.rem(x + 4 - kx, 4)
            at = pl.ds(pl.multiple_of(src * 16, 16), 16)
            for m in range(7):
                w[m, at, :] = groups[ky][kx, m]
    u = root[...]
    for k in range(4):
        left = split(u)
        c[k] = dot2(left, w[2 * k + 1 if k < 3 else 6])
        if k < 3:
            u = dot2(left, w[2 * k])


def chain(root, groups):
    return pl.pallas_call(
        chain_kernel,
        out_shape=(jax.ShapeDtypeStruct((4, 8, 256), F32), jax.ShapeDtypeStruct((7, 256, 256), BF)),
        in_specs=[VM] * 5,
        out_specs=(VM, VM),
        compiler_params=pltpu.CompilerParams(vmem_limit_bytes=8 * MB),
        name="chain",
    )(root, *groups)


def swapped(value, bit):
    return lax.ppermute(value, "leaf", [(i, i ^ (1 << bit)) for i in range(16)])


def shards(points, values, order, block_list, leaf_basis, local_transfers, chain_transfers):
    shard = chain_transfers[0].reshape(8, 16, 256)
    shard = jnp.concatenate([shard[:6], shard[7:]], 0)
    row = [shard] + [
        lax.ppermute(shard, "probe", [(i, i // 4 * 4 + (i + k) % 4) for i in range(16)])
        for k in range(1, 4)
    ]
    row = jnp.stack(row)
    groups = [row] + [
        lax.ppermute(row, "probe", [(i, (i + 4 * k) % 16) for i in range(16)]) for k in range(1, 4)
    ]
    own = tree(points, values, order)
    left = lax.ppermute(own, "leaf", [(i, (i + 1) % 16) for i in range(16)])
    right = lax.ppermute(own, "leaf", [(i, (i - 1) % 16) for i in range(16)])
    slots = block_list - (lax.axis_index("leaf") * 16 - 16)
    g, root = up(own, leaf_basis, local_transfers)
    near_f = near(slots, left, own, right)
    c, w = chain(root, groups)
    c = c[:, :4]
    cf = []
    for k in range(4):
        other = swapped(c, k)
        cf.append(other[0])
        c = c[1:] + other[1:]
    cf = jnp.stack(cf)
    cf = jnp.concatenate([cf, jnp.zeros_like(cf)], 1)
    return down(order, cf, near_f, g, w, leaf_basis, local_transfers)


def solution(mesh):
    placed = (
        P(None, "leaf"),
        P("probe", "leaf"),
        P("leaf", None),
        P("leaf", None),
        P("leaf", None, None),
        P("leaf", None, None, None, None),
        P("leaf", None, None, "probe", None),
    )
    return jax.shard_map(
        shards, mesh=mesh, in_specs=placed, out_specs=P("probe", "leaf"), check_vma=False
    )
```

time: 644 us -> 72.7 us (0.11)
  the two profiles are of different devices: /device:TPU:24 before, /device:TPU:14 now
where the time goes in v1:
time: 72.7 us; the launch traced here: 72.1 us
  Pallas kernels  26.3 us (36%)
  starting transfers between devices  21.8 us (30%)
  local copies, waits for them, and re-layouts  14.7 us (20%)
  waiting for transfers between devices  8.36 us (11%)
  other arithmetic  0.75 us (1%)
    pallas_call x1, Pallas kernels, near(): pl.pallas_call(functools.partial(near_kernel, variant, recip, unroll), ou...  16 us
    unnamed x21, local copies, waits for them, and re-layouts  11.7 us
    ppermute x4, starting transfers between devices, swapped(): return lax.ppermute(value, 'leaf', [(i, i ^ 1 << bit) for i in range(16)])  10.9 us
    pallas_call x1, Pallas kernels, down(): pl.pallas_call(down_kernel, out_shape=jax.ShapeDtypeStruct((4, 4096), F32...  5.42 us
    ppermute x3, waiting for transfers between devices, shards(): lax.ppermute(shard, 'probe', [(i, i // 4 * 4 + (i + k) % 4) for i in rang...  5.38 us
    ppermute x3, starting transfers between devices, shards(): lax.ppermute(row, 'probe', [(i, (i + 4 * k) % 16) for i in range(16)])  5 us
    ppermute x3, starting transfers between devices, shards(): lax.ppermute(shard, 'probe', [(i, i // 4 * 4 + (i + k) % 4) for i in rang...  3.59 us
    pallas_call x1, Pallas kernels, up(): pl.pallas_call(up_kernel, out_shape=(jax.ShapeDtypeStruct((30, 8, 256), F...  3.18 us
  transfers between devices with their start and end apart: 12, of which 4 were waited for; matrix products, arithmetic and copies ran while one was open for 4% of the time, Pallas kernels for 28%

profile of v1, /device:TPU:14, one launch (start us, length us, event | category | flops | bytes accessed | tf_op | source)
XLA Modules:
  0.0 72.1 jit_solution(11695961508485884466)
XLA Ops:
  0.0 0.8 %slice.40 = bf16[1,3,2,16,256]{4,3,2,1,0:T(8,128)(2,1)S(1)} slice(bf16[1,4,2,16,256]{4,3,2,1,0:T(8,128)(2,1)} %param.13), slice={[0:1], [0:3], [0:2], [0:16], [0:256]} | slice | bytes 98304 | tf_op jit(solution)/shard_map/slice | solution.py:297
  0.8 0.7 slice.53
  1.5 1.5 %collective-permute-start.1 = (bf16[7,16,256]{2,1,0:T(8,128)(2,1)S(1)}, bf16[7,16,256]{2,1,0:T(8,128)(2,1)S(1)}, u32[]{:S(2)}, u32[]{:S(2)}) collective-permute-start(bf16[7,16,256]{2,1,0:T(8,128)(2,1)S(1)} %get-tuple-element.14), channel_id=1, source_target_pairs={{0,2},{1,3},{2,0},{3,1},{4,6},{5,7},{6,4},{7,5},{8,10},{9,11},{10,... | collective-permute-start | bytes 172040 | tf_op jit(solution)/shard_map/ppermute | solution.py:299
  3.0 2.1 %collective-permute-start = (bf16[7,16,256]{2,1,0:T(8,128)(2,1)S(1)}, bf16[7,16,256]{2,1,0:T(8,128)(2,1)S(1)}, u32[]{:S(2)}, u32[]{:S(2)}) collective-permute-start(bf16[7,16,256]{2,1,0:T(8,128)(2,1)S(1)} %get-tuple-element.14), channel_id=1, source_target_pairs={{0,1},{1,2},{2,3},{3,0},{4,5},{5,6},{6,7},{7,4},{8,9},{9,10},{10,1... | collective-permute-start | bytes 172040 | tf_op jit(solution)/shard_map/ppermute | solution.py:299
  5.1 2.5 %collective-permute-done.1 = bf16[7,16,256]{2,1,0:T(8,128)(2,1)S(1)} collective-permute-done((bf16[7,16,256]{2,1,0:T(8,128)(2,1)S(1)}, bf16[7,16,256]{2,1,0:T(8,128)(2,1)S(1)}, u32[]{:S(2)}, u32[]{:S(2)}) %collective-permute-start.1) | collective-permute-done | bytes 57376 | tf_op jit(solution)/shard_map/ppermute | solution.py:299
  7.6 2.9 %collective-permute-done.2 = bf16[7,16,256]{2,1,0:T(8,128)(2,1)S(1)} collective-permute-done((bf16[7,16,256]{2,1,0:T(8,128)(2,1)S(1)}, bf16[7,16,256]{2,1,0:T(8,128)(2,1)S(1)}, u32[]{:S(2)}, u32[]{:S(2)}) %collective-permute-start.2) | collective-permute-done | bytes 57376 | tf_op jit(solution)/shard_map/ppermute | solution.py:299
  10.5 0.5 collective-permute-start.5
  11.1 2.6 %collective-permute-start.4 = (bf16[4,7,16,256]{3,2,1,0:T(8,128)(2,1)S(1)}, bf16[4,7,16,256]{3,2,1,0:T(8,128)(2,1)S(1)}, u32[]{:S(2)}, u32[]{:S(2)}) collective-permute-start(bf16[4,7,16,256]{3,2,1,0:T(8,128)(2,1)S(1)} %pad_maximum_fusion.refs_1_), channel_id=1, source_target_pairs={{0,8},{1,9},{2,10},{3,11},{4,12},{5,13},{6,14},{7,15},{8,0},{9,1},... | collective-permute-start | bytes 688136 | tf_op jit(solution)/shard_map/ppermute | solution.py:304
  13.7 1.9 %collective-permute-start.3 = (bf16[4,7,16,256]{3,2,1,0:T(8,128)(2,1)S(1)}, bf16[4,7,16,256]{3,2,1,0:T(8,128)(2,1)S(1)}, u32[]{:S(2)}, u32[]{:S(2)}) collective-permute-start(bf16[4,7,16,256]{3,2,1,0:T(8,128)(2,1)S(1)} %pad_maximum_fusion.refs_1_), channel_id=1, source_target_pairs={{0,4},{1,5},{2,6},{3,7},{4,8},{5,9},{6,10},{7,11},{8,12},{9,13},{1... | collective-permute-start | bytes 688136 | tf_op jit(solution)/shard_map/ppermute | solution.py:304
  15.6 0.7 copy-done.4
  16.3 0.8 %copy-done.6 = bf16[8,4096]{1,0:T(8,128)(2,1)S(1)} copy-done((bf16[8,4096]{1,0:T(8,128)(2,1)S(1)}, bf16[8,4096]{1,0:T(8,128)(2,1)}, u32[]{:S(2)}) %copy-start.6) | copy-done | bytes 65560
  17.1 0.8 %copy-done.7 = bf16[4,4096]{1,0:T(4,128)(2,1)S(1)} copy-done((bf16[4,4096]{1,0:T(4,128)(2,1)S(1)}, bf16[4,4096]{1,0:T(4,128)(2,1)}, u32[]{:S(2)}) %copy-start.7) | copy-done | bytes 32792
  17.9 1.1 %tree.1.td.own = bf16[16,16,256]{2,1,0:T(8,128)(2,1)S(1)} custom-call(bf16[8,4096]{1,0:T(8,128)(2,1)S(1)} %copy-done.6, bf16[4,4096]{1,0:T(4,128)(2,1)S(1)} %copy-done.7, s32[1,4096]{1,0:T(1,128)S(1)} %copy-done.4), custom_call_target="tpu_custom_call" | custom-call | tf_op jit(solution)/shard_map/tree/pallas_call | solution.py:58
  19.0 3.2 %copy-done = bf16[1,30,2,256,256]{4,3,2,1,0:T(8,128)(2,1)S(1)} copy-done((bf16[1,30,2,256,256]{4,3,2,1,0:T(8,128)(2,1)S(1)}, bf16[1,30,2,256,256]{4,3,2,1,0:T(8,128)(2,1)}, u32[]{:S(2)}) %copy-start) | copy-done | bytes 7864344
  22.2 1.6 %copy-done.2 = bf16[16,256,256]{2,1,0:T(8,128)(2,1)S(1)} copy-done((bf16[16,256,256]{2,1,0:T(8,128)(2,1)S(1)}, bf16[16,256,256]{2,1,0:T(8,128)(2,1)}, u32[]{:S(2)}) %copy-start.2) | copy-done | bytes 2097176
  23.8 3.2 %up.1 = (f32[30,8,256]{2,1,0:T(8,128)S(1)}, f32[8,256]{1,0:T(8,128)S(1)}) custom-call(bf16[16,16,256]{2,1,0:T(8,128)(2,1)S(1)} %tree.1.td.own, bf16[16,256,256]{2,1,0:T(8,128)(2,1)S(1)} %copy-done.2, bf16[1,30,2,256,256]{4,3,2,1,0:T(8,128)(2,1)S(1)} %copy-done), custom_call_target="tpu_custom_call" | custom-call | tf_op jit(solution)/shard_map/up/pallas_call | solution.py:109
  27.0 0.6 chain.1
  27.6 0.0 collective-permute-start.6
  27.6 1.2 %collective-permute-done.6 = f32[4,4,256]{2,1,0:T(4,128)S(1)} collective-permute-done((f32[4,4,256]{2,1,0:T(4,128)S(1)}, f32[4,4,256]{2,1,0:T(4,128)S(1)}, u32[]{:S(2)}, u32[]{:S(2)}) %collective-permute-start.6) | collective-permute-done | bytes 16416 | tf_op jit(solution)/shard_map/ppermute | solution.py:292
  28.8 2.0 %collective-permute-start.7 = (f32[3,4,256]{2,1,0:T(4,128)S(1)}, f32[3,4,256]{2,1,0:T(4,128)S(1)}, u32[]{:S(2)}, u32[]{:S(2)}) collective-permute-start(f32[3,4,256]{2,1,0:T(4,128)S(1)} %slice_add_fusion), channel_id=1, source_target_pairs={{0,32},{16,48},{32,0},{48,16},{64,96},{80,112},{96,64},{112,80},{1... | collective-permute-start | bytes 36872 | tf_op jit(solution)/shard_map/ppermute | solution.py:292
  30.8 1.8 %collective-permute-done.7 = f32[3,4,256]{2,1,0:T(4,128)S(1)} collective-permute-done((f32[3,4,256]{2,1,0:T(4,128)S(1)}, f32[3,4,256]{2,1,0:T(4,128)S(1)}, u32[]{:S(2)}, u32[]{:S(2)}) %collective-permute-start.7) | collective-permute-done | bytes 12320 | tf_op jit(solution)/shard_map/ppermute | solution.py:292
  32.6 0.6 copy-done.9
  33.2 3.3 %collective-permute-start.8 = (f32[2,4,256]{2,1,0:T(4,128)S(1)}, f32[2,4,256]{2,1,0:T(4,128)}, u32[]{:S(2)}, u32[]{:S(2)}) collective-permute-start(f32[2,4,256]{2,1,0:T(4,128)S(1)} %slice_add_fusion.1), channel_id=1, source_target_pairs={{0,64},{16,80},{32,96},{48,112},{64,0},{80,16},{96,32},{112,48},{1... | collective-permute-start | bytes 24584 | tf_op jit(solution)/shard_map/ppermute | solution.py:292
  36.5 2.3 %collective-permute-start.11 = (bf16[16,16,256]{2,1,0:T(8,128)(2,1)S(1)}, bf16[16,16,256]{2,1,0:T(8,128)(2,1)S(1)}, u32[]{:S(2)}, u32[]{:S(2)}) collective-permute-start(bf16[16,16,256]{2,1,0:T(8,128)(2,1)S(1)} %tree.1.td.own), channel_id=1, source_target_pairs={{0,240},{16,0},{32,16},{48,32},{64,48},{80,64},{96,80},{112,96},{1... | collective-permute-start | bytes 393224 | tf_op jit(solution)/shard_map/ppermute | solution.py:308
  38.8 0.8 %copy.9 = s32[16,8]{1,0:T(8,128)S(1)} copy(s32[16,8]{0,1:T(8,128)} %param.10) | data formatting | bytes 1024 | tf_op args[3]
  39.5 0.7 fusion.1
  40.2 5.6 %collective-permute-start.9 = (f32[1,4,256]{2,1,0:T(4,128)S(1)}, f32[1,4,256]{2,1,0:T(4,128)S(1)}, u32[]{:S(2)}, u32[]{:S(2)}) collective-permute-start(f32[1,4,256]{2,1,0:T(4,128)S(1)} %get-tuple-element.16), channel_id=1, source_target_pairs={{0,128},{16,144},{32,160},{48,176},{64,192},{80,208},{96,224},{112... | collective-permute-start | bytes 12296 | tf_op jit(solution)/shard_map/ppermute | solution.py:292
  45.9 16.0 %near.1.near_f = f32[16,8,256]{2,1,0:T(8,128)S(1)} custom-call(s32[16,8]{1,0:T(8,128)S(1)} %broadcast_subtract_fusion.slots, bf16[16,16,256]{2,1,0:T(8,128)(2,1)} %collective-permute-done.10.left, bf16[16,16,256]{2,1,0:T(8,128)(2,1)S(1)} %tree.1.td.own, bf16[16,16,256]{2,1,0:T(8,128)(2,1)S(1)} %collective-permute-done.11.right), custom_call_target="tpu_custom_call" | custom-call | tf_op jit(solution)/shard_map/near/pallas_call | solution.py:178
  61.9 0.8 %slice.54 = f32[1,4,256]{2,1,0:T(4,128)S(1)} slice(f32[4,4,256]{2,1,0:T(4,128)} %copy-done.8), slice={[0:1], [0:4], [0:256]} | slice | bytes 8192 | tf_op jit(solution)/shard_map/slice | solution.py:317
  62.7 0.7 slice.56
  63.4 3.2 %copy-done.1 = bf16[1,30,2,256,256]{4,3,2,1,0:T(8,128)(2,1)S(1)} copy-done((bf16[1,30,2,256,256]{4,3,2,1,0:T(8,128)(2,1)S(1)}, bf16[1,30,2,256,256]{4,3,2,1,0:T(8,128)(2,1)}, u32[]{:S(2)}) %copy-start.1) | copy-done | bytes 7864344
  66.7 5.4 %down.1 = f32[4,4096]{1,0:T(4,128)} custom-call(s32[1,4096]{1,0:T(1,128)S(1)} %copy-done.5, f32[4,8,256]{2,1,0:T(8,128)S(1)} %select_maximum_fusion.cf, f32[16,8,256]{2,1,0:T(8,128)S(1)} %near.1.near_f, f32[30,8,256]{2,1,0:T(8,128)S(1)} %get-tuple-element.11.g, bf16[7,256,256]{2,1,0:T(8,128)(2,1)S(1)} %get-tuple-element.12.chain, ...), custom_call_target="tpu_custom_call" | custom-call | tf_op jit(solution)/shard_map/down/pallas_call | solution.py:245
  (30 shorter events, 0.1 us)
Async XLA Ops:
  0.0 63.4 %copy-start.5 = (s32[1,4096]{1,0:T(1,128)S(1)}, s32[1,4096]{1,0:T(1,128)}, u32[]{:S(2)}) copy-start(s32[1,4096]{1,0:T(1,128)} %order.3) | copy-start | bytes 49156
  1.5 6.0 %collective-permute-start.1 = (bf16[7,16,256]{2,1,0:T(8,128)(2,1)S(1)}, bf16[7,16,256]{2,1,0:T(8,128)(2,1)S(1)}, u32[]{:S(2)}, u32[]{:S(2)}) collective-permute-start(bf16[7,16,256]{2,1,0:T(8,128)(2,1)S(1)} %get-tuple-element.14), channel_id=1, source_target_pairs={{0,2},{1,3},{2,0},{3,1},{4,6},{5,7},{6,4},{7,5},{8,10},{9,11},{10,... | collective-permute-start | bytes 172040 | tf_op jit(solution)/shard_map/ppermute | solution.py:299
  3.0 4.6 %collective-permute-start = (bf16[7,16,256]{2,1,0:T(8,128)(2,1)S(1)}, bf16[7,16,256]{2,1,0:T(8,128)(2,1)S(1)}, u32[]{:S(2)}, u32[]{:S(2)}) collective-permute-start(bf16[7,16,256]{2,1,0:T(8,128)(2,1)S(1)} %get-tuple-element.14), channel_id=1, source_target_pairs={{0,1},{1,2},{2,3},{3,0},{4,5},{5,6},{6,7},{7,4},{8,9},{9,10},{10,1... | collective-permute-start | bytes 172040 | tf_op jit(solution)/shard_map/ppermute | solution.py:299
  5.1 5.4 %collective-permute-start.2 = (bf16[7,16,256]{2,1,0:T(8,128)(2,1)S(1)}, bf16[7,16,256]{2,1,0:T(8,128)(2,1)S(1)}, u32[]{:S(2)}, u32[]{:S(2)}) collective-permute-start(bf16[7,16,256]{2,1,0:T(8,128)(2,1)S(1)} %get-tuple-element.14), channel_id=1, source_target_pairs={{0,3},{1,0},{2,1},{3,2},{4,7},{5,4},{6,5},{7,6},{8,11},{9,8},{10,9... | collective-permute-start | bytes 172040 | tf_op jit(solution)/shard_map/ppermute | solution.py:299
  10.5 16.5 %collective-permute-start.5 = (bf16[4,7,16,256]{3,2,1,0:T(8,128)(2,1)S(1)}, bf16[4,7,16,256]{3,2,1,0:T(8,128)(2,1)S(1)}, u32[]{:S(2)}, u32[]{:S(2)}) collective-permute-start(bf16[4,7,16,256]{3,2,1,0:T(8,128)(2,1)S(1)} %pad_maximum_fusion.refs_1_), channel_id=1, source_target_pairs={{0,12},{1,13},{2,14},{3,15},{4,0},{5,1},{6,2},{7,3},{8,4},{9,5},{1... | collective-permute-start | bytes 688136 | tf_op jit(solution)/shard_map/ppermute | solution.py:304
  11.1 15.9 %collective-permute-start.4 = (bf16[4,7,16,256]{3,2,1,0:T(8,128)(2,1)S(1)}, bf16[4,7,16,256]{3,2,1,0:T(8,128)(2,1)S(1)}, u32[]{:S(2)}, u32[]{:S(2)}) collective-permute-start(bf16[4,7,16,256]{3,2,1,0:T(8,128)(2,1)S(1)} %pad_maximum_fusion.refs_1_), channel_id=1, source_target_pairs={{0,8},{1,9},{2,10},{3,11},{4,12},{5,13},{6,14},{7,15},{8,0},{9,1},... | collective-permute-start | bytes 688136 | tf_op jit(solution)/shard_map/ppermute | solution.py:304
  13.7 13.4 %collective-permute-start.3 = (bf16[4,7,16,256]{3,2,1,0:T(8,128)(2,1)S(1)}, bf16[4,7,16,256]{3,2,1,0:T(8,128)(2,1)S(1)}, u32[]{:S(2)}, u32[]{:S(2)}) collective-permute-start(bf16[4,7,16,256]{3,2,1,0:T(8,128)(2,1)S(1)} %pad_maximum_fusion.refs_1_), channel_id=1, source_target_pairs={{0,4},{1,5},{2,6},{3,7},{4,8},{5,9},{6,10},{7,11},{8,12},{9,13},{1... | collective-permute-start | bytes 688136 | tf_op jit(solution)/shard_map/ppermute | solution.py:304
  15.5 0.7 copy-start.4
  16.3 0.8 %copy-start.6 = (bf16[8,4096]{1,0:T(8,128)(2,1)S(1)}, bf16[8,4096]{1,0:T(8,128)(2,1)}, u32[]{:S(2)}) copy-start(bf16[8,4096]{1,0:T(8,128)(2,1)} %points.1) | copy-start | bytes 196612
  17.1 0.8 %copy-start.7 = (bf16[4,4096]{1,0:T(4,128)(2,1)S(1)}, bf16[4,4096]{1,0:T(4,128)(2,1)}, u32[]{:S(2)}) copy-start(bf16[4,4096]{1,0:T(4,128)(2,1)} %values.1) | copy-start | bytes 98308
  19.0 3.2 %copy-start = (bf16[1,30,2,256,256]{4,3,2,1,0:T(8,128)(2,1)S(1)}, bf16[1,30,2,256,256]{4,3,2,1,0:T(8,128)(2,1)}, u32[]{:S(2)}) copy-start(bf16[1,30,2,256,256]{4,3,2,1,0:T(8,128)(2,1)} %lt.3) | copy-start | bytes 23592964
  22.2 1.6 %copy-start.2 = (bf16[16,256,256]{2,1,0:T(8,128)(2,1)S(1)}, bf16[16,256,256]{2,1,0:T(8,128)(2,1)}, u32[]{:S(2)}) copy-start(bf16[16,256,256]{2,1,0:T(8,128)(2,1)} %basis.3) | copy-start | bytes 6291460
  23.8 39.6 %copy-start.3 = (bf16[16,256,256]{2,1,0:T(8,128)(2,1)S(1)}, bf16[16,256,256]{2,1,0:T(8,128)(2,1)}, u32[]{:S(2)}) copy-start(bf16[16,256,256]{2,1,0:T(8,128)(2,1)} %basis.3) | copy-start | bytes 6291460
  27.6 1.2 %collective-permute-start.6 = (f32[4,4,256]{2,1,0:T(4,128)S(1)}, f32[4,4,256]{2,1,0:T(4,128)S(1)}, u32[]{:S(2)}, u32[]{:S(2)}) collective-permute-start(f32[4,4,256]{2,1,0:T(4,128)S(1)} %slice.43), channel_id=1, source_target_pairs={{0,16},{16,0},{32,48},{48,32},{64,80},{80,64},{96,112},{112,96},{1... | collective-permute-start | bytes 49160 | tf_op jit(solution)/shard_map/ppermute | solution.py:292
  28.8 7.7 %copy-start.8 = (f32[4,4,256]{2,1,0:T(4,128)}, f32[4,4,256]{2,1,0:T(4,128)S(1)}, u32[]{:S(2)}) copy-start(f32[4,4,256]{2,1,0:T(4,128)S(1)} %collective-permute-done.6) | copy-start | bytes 49156
  28.8 3.8 %collective-permute-start.7 = (f32[3,4,256]{2,1,0:T(4,128)S(1)}, f32[3,4,256]{2,1,0:T(4,128)S(1)}, u32[]{:S(2)}, u32[]{:S(2)}) collective-permute-start(f32[3,4,256]{2,1,0:T(4,128)S(1)} %slice_add_fusion), channel_id=1, source_target_pairs={{0,32},{16,48},{32,0},{48,16},{64,96},{80,112},{96,64},{112,80},{1... | collective-permute-start | bytes 36872 | tf_op jit(solution)/shard_map/ppermute | solution.py:292
  32.6 0.6 copy-start.9
  33.2 6.3 %collective-permute-start.8 = (f32[2,4,256]{2,1,0:T(4,128)S(1)}, f32[2,4,256]{2,1,0:T(4,128)}, u32[]{:S(2)}, u32[]{:S(2)}) collective-permute-start(f32[2,4,256]{2,1,0:T(4,128)S(1)} %slice_add_fusion.1), channel_id=1, source_target_pairs={{0,64},{16,80},{32,96},{48,112},{64,0},{80,16},{96,32},{112,48},{1... | collective-permute-start | bytes 24584 | tf_op jit(solution)/shard_map/ppermute | solution.py:292
  36.5 9.4 %collective-permute-start.11 = (bf16[16,16,256]{2,1,0:T(8,128)(2,1)S(1)}, bf16[16,16,256]{2,1,0:T(8,128)(2,1)S(1)}, u32[]{:S(2)}, u32[]{:S(2)}) collective-permute-start(bf16[16,16,256]{2,1,0:T(8,128)(2,1)S(1)} %tree.1.td.own), channel_id=1, source_target_pairs={{0,240},{16,0},{32,16},{48,32},{64,48},{80,64},{96,80},{112,96},{1... | collective-permute-start | bytes 393224 | tf_op jit(solution)/shard_map/ppermute | solution.py:308
  38.8 7.1 %collective-permute-start.10 = (bf16[16,16,256]{2,1,0:T(8,128)(2,1)S(1)}, bf16[16,16,256]{2,1,0:T(8,128)(2,1)}, u32[]{:S(2)}, u32[]{:S(2)}) collective-permute-start(bf16[16,16,256]{2,1,0:T(8,128)(2,1)S(1)} %tree.1.td.own), channel_id=1, source_target_pairs={{0,16},{16,32},{32,48},{48,64},{64,80},{80,96},{96,112},{112,128},... | collective-permute-start | bytes 393224 | tf_op jit(solution)/shard_map/ppermute | solution.py:307
  40.2 23.2 %collective-permute-start.9 = (f32[1,4,256]{2,1,0:T(4,128)S(1)}, f32[1,4,256]{2,1,0:T(4,128)S(1)}, u32[]{:S(2)}, u32[]{:S(2)}) collective-permute-start(f32[1,4,256]{2,1,0:T(4,128)S(1)} %get-tuple-element.16), channel_id=1, source_target_pairs={{0,128},{16,144},{32,160},{48,176},{64,192},{80,208},{96,224},{112... | collective-permute-start | bytes 12296 | tf_op jit(solution)/shard_map/ppermute | solution.py:292
  63.4 3.2 %copy-start.1 = (bf16[1,30,2,256,256]{4,3,2,1,0:T(8,128)(2,1)S(1)}, bf16[1,30,2,256,256]{4,3,2,1,0:T(8,128)(2,1)}, u32[]{:S(2)}) copy-start(bf16[1,30,2,256,256]{4,3,2,1,0:T(8,128)(2,1)} %lt.3) | copy-start | bytes 23592964

commit v2 on v1

v2 whole, which is shorter than its diff:
```python
import functools
import jax
import jax.numpy as jnp
from jax import lax
from jax.experimental import pallas as pl
from jax.experimental.pallas import tpu as pltpu
from jax.sharding import PartitionSpec as P

F32 = jnp.float32
BF = jnp.bfloat16
MB = 2**20
NT = (((1,), (1,)), ((), ()))
NN = (((1,), (0,)), ((), ()))
VM = pl.BlockSpec(memory_space=pltpu.VMEM)
SM = pl.BlockSpec(memory_space=pltpu.SMEM)
HBM = pl.BlockSpec(memory_space=pltpu.HBM)


def dot(a, b, dims=NN):
    return lax.dot_general(a, b, dims, preferred_element_type=F32)


def split(s):
    hi = s.astype(BF).astype(F32)
    return jnp.concatenate([hi, s - hi], 0).astype(BF)


def dot2(left, mat, dims=NN):
    r = dot(left, mat, dims)
    return r[:8] + r[8:]


LEVELS = ((0, 16), (16, 8), (24, 4), (28, 2))


def starter(sem):
    copies = []

    def start(src, dst):
        copy = pltpu.make_async_copy(src, dst, sem.at[len(copies)])
        copy.start()
        copies.append(copy)

    return copies, start


def up_kernel(points, values, order, basis, lt, td, g, root, pv, vv, ov, xs, xr, bas, ltv, s, sem):
    copies, start = starter(sem)
    start(points, pv)
    start(values, vv)
    start(order, ov)
    for q in range(2):
        start(basis.at[pl.ds(q * 8, 8)], bas.at[pl.ds(q * 8, 8)])
    for q in range(4):
        start(lt.at[0, pl.ds(q * 4, 4)], ltv.at[pl.ds(q * 4, 4)])
    for q in range(2):
        start(lt.at[0, pl.ds(16 + q * 4, 4)], ltv.at[pl.ds(16 + q * 4, 4)])
    start(lt.at[0, pl.ds(24, 6)], ltv.at[pl.ds(24, 6)])
    for copy in copies[:3]:
        copy.wait()
    xs[0:8, :] = pv[...].astype(F32)
    xs[8:16, :] = jnp.zeros((8, xs.shape[1]), F32)
    xs[8:12, :] = vv[...].astype(F32)
    for h in range(16):
        xr[h * 16 : h * 16 + 16, :] = xs[:, h * 256 : h * 256 + 256].astype(BF)
    rows = lax.broadcasted_iota(jnp.int32, (256, 256), 0)
    sub = lax.broadcasted_iota(jnp.int32, (8, 256), 0)
    for t in range(16):
        o = ov[:, t * 256 : t * 256 + 256]
        oh = jnp.where(rows == (o & 255), 1.0, 0.0).astype(BF)
        z = dot(xr[...], oh)
        hi = o >> 8
        low = jnp.zeros((8, 256), F32)
        high = jnp.zeros((8, 256), F32)
        for h in range(16):
            low = jnp.where(hi == h, z[h * 16 : h * 16 + 8], low)
            high = jnp.where(hi == h, z[h * 16 + 8 : h * 16 + 16], high)
        m = jnp.sum(low * low, 0, keepdims=True) * 0.125
        mh = m.astype(BF).astype(F32)
        high = jnp.where(sub == 4, mh, jnp.where(sub == 5, m - mh, jnp.where(sub >= 6, 1.0, high)))
        td[t] = jnp.concatenate([low, high], 0).astype(BF)
    for l in range(16):
        if l % 8 == 0:
            copies[3 + l // 8].wait()
        r = dot(td[l], bas[l])
        s[l] = jnp.where(sub < 4, r[8:], 0.0)
    for start_slot, count in LEVELS:
        for n in range(0, count, 2):
            slot = start_slot + n
            if slot % 4 == 0 and slot < 24:
                copies[5 + slot // 4].wait()
            if slot == 24:
                copies[11].wait()
            l0 = split(s[n])
            l1 = split(s[n + 1])
            g[slot + 1] = dot2(l0, ltv[slot, 1])
            g[slot] = dot2(l1, ltv[slot + 1, 1])
            s[n // 2] = dot2(l0, ltv[slot, 0]) + dot2(l1, ltv[slot + 1, 0])
    root[...] = s[0]


def up(points, values, order, basis, lt):
    return pl.pallas_call(
        up_kernel,
        out_shape=(
            jax.ShapeDtypeStruct((16, 16, 256), BF),
            jax.ShapeDtypeStruct((30, 8, 256), F32),
            jax.ShapeDtypeStruct((8, 256), F32),
        ),
        in_specs=[HBM] * 5,
        out_specs=(VM, VM, VM),
        scratch_shapes=[
            pltpu.VMEM((8, 4096), BF),
            pltpu.VMEM((4, 4096), BF),
            pltpu.VMEM((1, 4096), jnp.int32),
            pltpu.VMEM((16, 4096), F32),
            pltpu.VMEM((256, 256), BF),
            pltpu.VMEM((16, 256, 256), BF),
            pltpu.VMEM((30, 2, 256, 256), BF),
            pltpu.VMEM((16, 8, 256), F32),
            pltpu.SemaphoreType.DMA((12,)),
        ],
        compiler_params=pltpu.CompilerParams(vmem_limit_bytes=16 * MB),
        name="up",
    )(points, values, order, basis, lt)


def sources(ref):
    p = ref[...].astype(F32)
    sub = lax.broadcasted_iota(jnp.int32, (16, 256), 0)
    m = jnp.sum(jnp.where(sub < 8, p * p, 0.0), 0, keepdims=True) * 0.125 + 1.0
    mh = m.astype(BF).astype(F32)
    p = jnp.where(
        sub < 8,
        p * -0.25,
        jnp.where(sub < 12, 0.0, jnp.where(sub < 14, 1.0, jnp.where(sub == 14, mh, m - mh))),
    )
    return p.T.astype(BF)


def block(pt, q):
    f = dot(pt, q)
    return dot(q, pltpu.reciprocal(f * f * f, approx=True).astype(BF), NT)[8:]


def near_own_kernel(own, out, pt):
    for l in range(16):
        pt[l] = sources(own.at[l])
        out[l] = block(pt[l], own[l])


def near_own(own):
    return pl.pallas_call(
        near_own_kernel,
        out_shape=(
            jax.ShapeDtypeStruct((16, 8, 256), F32),
            jax.ShapeDtypeStruct((16, 256, 16), BF),
        ),
        in_specs=[VM],
        out_specs=(VM, VM),
        compiler_params=pltpu.CompilerParams(vmem_limit_bytes=4 * MB),
        name="near_own",
    )(own)


def near_kernel(first, count, slot_ref, left, own, right, base, pt, out, win):
    slots = slot_ref[...]
    win[0:16] = left[...]
    win[16:32] = own[...]
    win[32:48] = right[...]
    for l in range(first, first + count):
        total = base[l]
        for n in range(1, 8):
            total = total + block(pt[l], win[slots[l, n]])
        out[l - first] = total


def near(first, count, slots, left, own, right, base, pt):
    return pl.pallas_call(
        functools.partial(near_kernel, first, count),
        out_shape=jax.ShapeDtypeStruct((count, 8, 256), F32),
        in_specs=[VM] * 6,
        out_specs=VM,
        scratch_shapes=[pltpu.VMEM((48, 16, 256), BF)],
        compiler_params=pltpu.CompilerParams(vmem_limit_bytes=8 * MB),
        name="near",
    )(slots, left, own, right, base, pt)


R1 = ((0, 0), (2, 0), (1, 2), (3, 2))
R2 = ((0, 0), (0, 1), (0, 3), (1, 0))


def shifted(value, shift):
    pairs = [
        (y * 4 + x, (y + shift[0]) % 4 * 4 + (x + shift[1]) % 4) for y in range(4) for x in range(4)
    ]
    return lax.ppermute(value, "probe", pairs)


def chain_kernel(*refs):
    root, groups, c, w = refs[0], refs[1:5], refs[5], refs[6]
    me = lax.axis_index("probe")
    y, x = me // 4, lax.rem(me, 4)
    for ky in range(4):
        for kx in range(4):
            sy = lax.rem(y + 8 - R2[ky][0] - R1[kx][0], 4)
            sx = lax.rem(x + 8 - R2[ky][1] - R1[kx][1], 4)
            at = pl.ds(pl.multiple_of((sy * 4 + sx) * 16, 16), 16)
            for m in range(7):
                w[m, at, :] = groups[ky][kx, m]
    u = root[...]
    for k in range(4):
        left = split(u)
        c[k] = dot2(left, w[2 * k + 1 if k < 3 else 6])
        if k < 3:
            u = dot2(left, w[2 * k])


def chain(root, groups):
    return pl.pallas_call(
        chain_kernel,
        out_shape=(jax.ShapeDtypeStruct((4, 8, 256), F32), jax.ShapeDtypeStruct((7, 256, 256), BF)),
        in_specs=[VM] * 5,
        out_specs=(VM, VM),
        compiler_params=pltpu.CompilerParams(vmem_limit_bytes=8 * MB),
        name="chain",
    )(root, *groups)


def down_kernel(
    order, o1, q1, q2, q3, o3, na, nb, nc, g, chain, basis, lt, out, ov, bas, ltv, f, ohs, sem
):
    copies, start = starter(sem)
    start(order, ov)
    start(lt.at[0, pl.ds(24, 6), 0], ltv.at[pl.ds(24, 6)])
    start(lt.at[0, pl.ds(16, 8), 0], ltv.at[pl.ds(16, 8)])
    for q in range(2):
        start(lt.at[0, pl.ds(8 * q, 8), 0], ltv.at[pl.ds(8 * q, 8)])
    for q in range(4):
        start(basis.at[pl.ds(q * 4, 4)], bas.at[pl.ds(q * 4, 4)])
    top = o3[0]
    for term, k in ((q2[0] + q3[0], 2), (q1[0], 1), (o1[0], 0)):
        top = term + dot2(split(top), chain[2 * k], NT)
    f[0] = top
    copies[0].wait()
    rows = lax.broadcasted_iota(jnp.int32, (256, 256), 0)
    for t in range(16):
        o = ov[:, t * 256 : t * 256 + 256]
        ohs[t] = jnp.where(rows == (o & 255), 1.0, 0.0).astype(BF)
    for start_slot, count in LEVELS[::-1]:
        if start_slot == 28:
            copies[1].wait()
        if start_slot == 16:
            copies[2].wait()
        if start_slot == 0:
            copies[3].wait()
            copies[4].wait()
        for m in range(count // 2 - 1, -1, -1):
            slot = start_slot + 2 * m
            l = split(f[m])
            f[2 * m + 1] = g[slot + 1] + dot2(l, ltv[slot + 1], NT)
            f[2 * m] = g[slot] + dot2(l, ltv[slot], NT)
    near_f = [r[i] for r in (na, nb, nc) for i in range(r.shape[0])]
    hrow = lax.broadcasted_iota(jnp.int32, (16, 256), 0)
    acc = jnp.zeros((128, 256), F32)
    for t in range(16):
        if t % 4 == 0:
            copies[5 + t // 4].wait()
        c = near_f[t] + dot2(split(f[t]), bas[t], NT)
        hit = hrow == (ov[:, t * 256 : t * 256 + 256] >> 8)
        ch = c.astype(BF).astype(F32)
        cl = c - ch
        parts = [jnp.where(hit, part[k : k + 1], 0.0) for k in range(4) for part in (ch, cl)]
        acc = acc + dot(jnp.concatenate(parts, 0).astype(BF), ohs[t], NT)
    for k in range(4):
        both = acc[k * 32 : k * 32 + 16] + acc[k * 32 + 16 : k * 32 + 32]
        for h in range(16):
            out[k : k + 1, h * 256 : h * 256 + 256] = both[h : h + 1]


def down(order, parts, g, w, basis, lt):
    return pl.pallas_call(
        down_kernel,
        out_shape=jax.ShapeDtypeStruct((4, 4096), F32),
        in_specs=[HBM] + [VM] * 10 + [HBM] * 2,
        out_specs=VM,
        scratch_shapes=[
            pltpu.VMEM((1, 4096), jnp.int32),
            pltpu.VMEM((16, 256, 256), BF),
            pltpu.VMEM((30, 256, 256), BF),
            pltpu.VMEM((16, 8, 256), F32),
            pltpu.VMEM((16, 256, 256), BF),
            pltpu.SemaphoreType.DMA((9,)),
        ],
        compiler_params=pltpu.CompilerParams(vmem_limit_bytes=16 * MB),
        name="down",
    )(order, *parts, g, w, basis, lt)


def swapped(value, mask):
    return lax.ppermute(value, "leaf", [(i, i ^ mask) for i in range(16)])


def pinned(value):
    return pltpu.with_memory_space_constraint(value, pltpu.HBM)


def tie(*values):
    return lax.optimization_barrier(values)


def shards(points, values, order, block_list, leaf_basis, local_transfers, chain_transfers):
    points, values, order, leaf_basis, local_transfers = map(
        pinned, (points, values, order, leaf_basis, local_transfers)
    )
    shard = chain_transfers.reshape(8, 16, 256)
    pair = shifted(shard, R1[1])
    own, g, root = up(points, values, order, leaf_basis, local_transfers)
    pair, own = tie(pair, own)
    pair = jnp.stack([shard, pair])
    other = shifted(pair, R1[2])
    left = lax.ppermute(own, "leaf", [(i, (i + 1) % 16) for i in range(16)])
    right = lax.ppermute(own, "leaf", [(i, (i - 1) % 16) for i in range(16)])
    base, pt = near_own(own)
    other, base, left, right = tie(other, base, left, right)
    row = jnp.concatenate([pair, other], 0)
    row = jnp.concatenate([row[:, :6], row[:, 7:]], 1)
    groups = [row] + [shifted(row, s) for s in R2[1:]]
    slots = block_list - (lax.axis_index("leaf") * 16 - 16)
    na = near(0, 8, slots, left, own, right, base, pt)
    *groups, na = tie(*groups, na)
    c, w = chain(root, groups)
    o1 = swapped(c, 1)
    s = c[1:] + o1[1:]
    q1 = swapped(s, 2)
    q2 = swapped(s[1:], 4)
    q3 = swapped(s[1:], 6)
    own, _ = tie(own, s)
    nb = near(8, 4, slots, left, own, right, base, pt)
    q1, q2, q3, nb = tie(q1, q2, q3, nb)
    last = s[2:] + q1[2:] + q2[1:] + q3[1:]
    o3 = swapped(last, 12)
    own, _ = tie(own, last)
    nc = near(12, 4, slots, left, own, right, base, pt)
    return down(order, (o1, q1, q2, q3, o3, na, nb, nc), g, w, leaf_basis, local_transfers)


def solution(mesh):
    placed = (
        P(None, "leaf"),
        P("probe", "leaf"),
        P("leaf", None),
        P("leaf", None),
        P("leaf", None, None),
        P("leaf", None, None, None, None),
        P("leaf", None, None, "probe", None),
    )
    return jax.shard_map(
        shards, mesh=mesh, in_specs=placed, out_specs=P("probe", "leaf"), check_vma=False
    )
```

time: 72.7 us -> 50.1 us (0.69)
  the two profiles are of different devices: /device:TPU:14 before, /device:TPU:24 now
where the time goes in v2:
time: 50.1 us; the launch traced here: 49.9 us
  Pallas kernels  20.8 us (42%)
  starting transfers between devices  20.7 us (41%)
  waiting for transfers between devices  7.94 us (16%)
    pallas_call x3, Pallas kernels, near(): pl.pallas_call(functools.partial(near_kernel, first, count), out_shape=ja...  8.93 us
    ppermute x5, starting transfers between devices, shifted(): return lax.ppermute(value, 'probe', pairs)  8.5 us
    ppermute x5, starting transfers between devices, swapped(): return lax.ppermute(value, 'leaf', [(i, i ^ mask) for i in range(16)])  7.45 us
    pallas_call x1, Pallas kernels, down(): pl.pallas_call(down_kernel, out_shape=jax.ShapeDtypeStruct((4, 4096), F32...  5.52 us
    ppermute x1, starting transfers between devices, shards(): right = lax.ppermute(own, 'leaf', [(i, (i - 1) % 16) for i in range(16)])  4.74 us
    pallas_call x1, Pallas kernels, up(): pl.pallas_call(up_kernel, out_shape=(jax.ShapeDtypeStruct((16, 16, 256),...  4.49 us
    ppermute x1, waiting for transfers between devices, shards(): left = lax.ppermute(own, 'leaf', [(i, (i + 1) % 16) for i in range(16)])  3.08 us
    ppermute x5, waiting for transfers between devices, shifted(): return lax.ppermute(value, 'probe', pairs)  2.13 us
  transfers between devices with their start and end apart: 12, of which 7 were waited for; matrix products, arithmetic and copies ran while one was open for 0% of the time, Pallas kernels for 30%

profile of v2, /device:TPU:24, one launch (start us, length us, event | category | flops | bytes accessed | tf_op | source)
XLA Modules:
  0.0 49.9 jit_solution(14241998747614932960)
XLA Ops:
  0.0 1.2 %collective-permute-start = (bf16[8,16,256]{2,1,0:T(8,128)(2,1)}, bf16[8,16,256]{2,1,0:T(8,128)(2,1)S(1)}, u32[]{:S(2)}, u32[]{:S(2)}) collective-permute-start(bf16[8,16,256]{2,1,0:T(8,128)(2,1)} %bitcast.3), channel_id=1, source_target_pairs={{0,8},{1,9},{2,10},{3,11},{4,12},{5,13},{6,14},{7,15},{8,0},{9,1},... | collective-permute-start | bytes 196616 | tf_op jit(solution)/shard_map/ppermute | solution.py:198
  1.2 4.5 %up.1 = (bf16[16,16,256]{2,1,0:T(8,128)(2,1)S(1)}, f32[30,8,256]{2,1,0:T(8,128)S(1)}, f32[8,256]{1,0:T(8,128)S(1)}) custom-call(bf16[8,4096]{1,0:T(8,128)(2,1)} %points.1, bf16[4,4096]{1,0:T(4,128)(2,1)} %values.1, s32[1,4096]{1,0:T(1,128)} %order.3, bf16[16,256,256]{2,1,0:T(8,128)(2,1)} %basis.3, bf16[1,30,2,256,256]{4,3,2,1,0:T(8,128)(2,1)} %lt.3), custom_call_target="tpu_custom_call" | custom-call | tf_op jit(solution)/shard_map/up/pallas_call | solution.py:103
  5.7 0.2 collective-permute-done
  6.0 4.5 %collective-permute-start.1 = (bf16[2,8,16,256]{3,2,1,0:T(8,128)(2,1)S(1)}, bf16[2,8,16,256]{3,2,1,0:T(8,128)(2,1)S(1)}, u32[]{:S(2)}, u32[]{:S(2)}) collective-permute-start(bf16[2,8,16,256]{3,2,1,0:T(8,128)(2,1)S(1)} %pad_maximum_fusion.1), channel_id=1, source_target_pairs={{0,6},{1,7},{2,4},{3,5},{4,10},{5,11},{6,8},{7,9},{8,14},{9,15},{1... | collective-permute-start | bytes 393224 | tf_op jit(solution)/shard_map/ppermute | solution.py:198
  10.5 4.7 %collective-permute-start.3 = (bf16[16,16,256]{2,1,0:T(8,128)(2,1)S(1)}, bf16[16,16,256]{2,1,0:T(8,128)(2,1)S(1)}, u32[]{:S(2)}, u32[]{:S(2)}) collective-permute-start(bf16[16,16,256]{2,1,0:T(8,128)(2,1)S(1)} %get-tuple-element.50.own), channel_id=1, source_target_pairs={{0,240},{16,0},{32,16},{48,32},{64,48},{80,64},{96,80},{112,96},{1... | collective-permute-start | bytes 393224 | tf_op jit(solution)/shard_map/ppermute | solution.py:324
  15.2 0.0 collective-permute-start.2
  15.2 1.3 %near_own.1 = (f32[16,8,256]{2,1,0:T(8,128)S(1)}, bf16[16,256,16]{2,1,0:T(8,128)(2,1)S(1)}) custom-call(bf16[16,16,256]{2,1,0:T(8,128)(2,1)S(1)} %get-tuple-element.50.own), custom_call_target="tpu_custom_call" | custom-call | tf_op jit(solution)/shard_map/near_own/pallas_call | solution.py:153
  16.6 0.0 collective-permute-done.1
  16.6 1.2 %collective-permute-done.3.right = bf16[16,16,256]{2,1,0:T(8,128)(2,1)S(1)} collective-permute-done((bf16[16,16,256]{2,1,0:T(8,128)(2,1)S(1)}, bf16[16,16,256]{2,1,0:T(8,128)(2,1)S(1)}, u32[]{:S(2)}, u32[]{:S(2)}) %collective-permute-start.3) | collective-permute-done | bytes 131104 | tf_op jit(solution)/shard_map/ppermute | solution.py:324
  17.8 3.1 %collective-permute-done.2.left = bf16[16,16,256]{2,1,0:T(8,128)(2,1)S(1)} collective-permute-done((bf16[16,16,256]{2,1,0:T(8,128)(2,1)S(1)}, bf16[16,16,256]{2,1,0:T(8,128)(2,1)S(1)}, u32[]{:S(2)}, u32[]{:S(2)}) %collective-permute-start.2) | collective-permute-done | bytes 131104 | tf_op jit(solution)/shard_map/ppermute | solution.py:323
  20.9 0.8 %collective-permute-start.6 = (bf16[4,7,16,256]{3,2,1,0:T(8,128)(2,1)S(1)}, bf16[4,7,16,256]{3,2,1,0:T(8,128)(2,1)S(1)}, u32[]{:S(2)}, u32[]{:S(2)}) collective-permute-start(bf16[4,7,16,256]{3,2,1,0:T(8,128)(2,1)S(1)} %fusion.5.refs_1_), channel_id=1, source_target_pairs={{0,4},{1,5},{2,6},{3,7},{4,8},{5,9},{6,10},{7,11},{8,12},{9,13},{1... | collective-permute-start | bytes 688136 | tf_op jit(solution)/shard_map/ppermute | solution.py:198
  21.7 1.1 %collective-permute-start.5 = (bf16[4,7,16,256]{3,2,1,0:T(8,128)(2,1)S(1)}, bf16[4,7,16,256]{3,2,1,0:T(8,128)(2,1)S(1)}, u32[]{:S(2)}, u32[]{:S(2)}) collective-permute-start(bf16[4,7,16,256]{3,2,1,0:T(8,128)(2,1)S(1)} %fusion.5.refs_1_), channel_id=1, source_target_pairs={{0,3},{1,0},{2,1},{3,2},{4,7},{5,4},{6,5},{7,6},{8,11},{9,8},{10,9... | collective-permute-start | bytes 688136 | tf_op jit(solution)/shard_map/ppermute | solution.py:198
  22.8 0.9 %collective-permute-start.4 = (bf16[4,7,16,256]{3,2,1,0:T(8,128)(2,1)S(1)}, bf16[4,7,16,256]{3,2,1,0:T(8,128)(2,1)S(1)}, u32[]{:S(2)}, u32[]{:S(2)}) collective-permute-start(bf16[4,7,16,256]{3,2,1,0:T(8,128)(2,1)S(1)} %fusion.5.refs_1_), channel_id=1, source_target_pairs={{0,1},{1,2},{2,3},{3,0},{4,5},{5,6},{6,7},{7,4},{8,9},{9,10},{10,1... | collective-permute-start | bytes 688136 | tf_op jit(solution)/shard_map/ppermute | solution.py:198
  23.7 0.1 copy.8
  23.8 4.4 %near.3.na = f32[8,8,256]{2,1,0:T(8,128)S(1)} custom-call(s32[16,8]{1,0:T(8,128)S(1)} %broadcast_subtract_fusion.slot_ref, bf16[16,16,256]{2,1,0:T(8,128)(2,1)S(1)} %collective-permute-done.2.left, bf16[16,16,256]{2,1,0:T(8,128)(2,1)S(1)} %get-tuple-element.50.own, bf16[16,16,256]{2,1,0:T(8,128)(2,1)S(1)} %collective-permute-done.3.right, ...), custom_call_target="tpu_custom_call" | custom-call | tf_op jit(solution)/shard_map/near/pallas_call | solution.py:179
  28.2 0.0 collective-permute-done.6.refs_4_
  28.2 0.1 collective-permute-done.5.refs_3_
  28.3 1.8 %collective-permute-done.4.refs_2_ = bf16[4,7,16,256]{3,2,1,0:T(8,128)(2,1)S(1)} collective-permute-done((bf16[4,7,16,256]{3,2,1,0:T(8,128)(2,1)S(1)}, bf16[4,7,16,256]{3,2,1,0:T(8,128)(2,1)S(1)}, u32[]{:S(2)}, u32[]{:S(2)}) %collective-permute-start.4) | collective-permute-done | bytes 229408 | tf_op jit(solution)/shard_map/ppermute | solution.py:198
  30.0 0.6 %chain.1 = (f32[4,8,256]{2,1,0:T(8,128)S(1)}, bf16[7,256,256]{2,1,0:T(8,128)(2,1)S(1)}) custom-call(f32[8,256]{1,0:T(8,128)S(1)} %get-tuple-element.29.refs_0_, bf16[4,7,16,256]{3,2,1,0:T(8,128)(2,1)S(1)} %fusion.5.refs_1_, bf16[4,7,16,256]{3,2,1,0:T(8,128)(2,1)S(1)} %collective-permute-done.4.refs_2_, ...), custom_call_target="tpu_custom_call" | custom-call | tf_op jit(solution)/shard_map/chain/pallas_call | solution.py:221
  30.6 0.2 collective-permute-start.7
  30.8 1.2 %collective-permute-done.7.o1 = f32[4,8,256]{2,1,0:T(8,128)S(1)} collective-permute-done((f32[4,8,256]{2,1,0:T(8,128)S(1)}, f32[4,8,256]{2,1,0:T(8,128)S(1)}, u32[]{:S(2)}, u32[]{:S(2)}) %collective-permute-start.7) | collective-permute-done | bytes 32800 | tf_op jit(solution)/shard_map/ppermute | solution.py:302
  32.0 0.0 collective-permute-start.8
  32.0 1.5 %collective-permute-start.10 = (f32[2,8,256]{2,1,0:T(8,128)S(1)}, f32[2,8,256]{2,1,0:T(8,128)S(1)}, u32[]{:S(2)}, u32[]{:S(2)}) collective-permute-start(f32[2,8,256]{2,1,0:T(8,128)S(1)} %slice.39), channel_id=1, source_target_pairs={{0,96},{16,112},{32,64},{48,80},{64,32},{80,48},{96,0},{112,16},{1... | collective-permute-start | bytes 49160 | tf_op jit(solution)/shard_map/ppermute | solution.py:302
  33.5 2.0 %collective-permute-start.9 = (f32[2,8,256]{2,1,0:T(8,128)S(1)}, f32[2,8,256]{2,1,0:T(8,128)S(1)}, u32[]{:S(2)}, u32[]{:S(2)}) collective-permute-start(f32[2,8,256]{2,1,0:T(8,128)S(1)} %slice.39), channel_id=1, source_target_pairs={{0,64},{16,80},{32,96},{48,112},{64,0},{80,16},{96,32},{112,48},{1... | collective-permute-start | bytes 49160 | tf_op jit(solution)/shard_map/ppermute | solution.py:302
  35.5 2.3 %near.4.nb = f32[4,8,256]{2,1,0:T(8,128)S(1)} custom-call(s32[16,8]{1,0:T(8,128)S(1)} %broadcast_subtract_fusion.slot_ref, bf16[16,16,256]{2,1,0:T(8,128)(2,1)S(1)} %collective-permute-done.2.left, bf16[16,16,256]{2,1,0:T(8,128)(2,1)S(1)} %get-tuple-element.50.own, bf16[16,16,256]{2,1,0:T(8,128)(2,1)S(1)} %collective-permute-done.3.right, ...), custom_call_target="tpu_custom_call" | custom-call | tf_op jit(solution)/shard_map/near/pallas_call | solution.py:179
  37.8 0.0 collective-permute-done.10.q3
  37.8 0.3 collective-permute-done.9.q2
  38.2 0.0 collective-permute-done.8.q1
  38.2 3.8 %collective-permute-start.11 = (f32[1,8,256]{2,1,0:T(8,128)S(1)}, f32[1,8,256]{2,1,0:T(8,128)S(1)}, u32[]{:S(2)}, u32[]{:S(2)}) collective-permute-start(f32[1,8,256]{2,1,0:T(8,128)S(1)} %fusion.7), channel_id=1, source_target_pairs={{0,192},{16,208},{32,224},{48,240},{64,128},{80,144},{96,160},{112... | collective-permute-start | bytes 24584 | tf_op jit(solution)/shard_map/ppermute | solution.py:302
  42.0 2.3 %near.5.nc = f32[4,8,256]{2,1,0:T(8,128)S(1)} custom-call(s32[16,8]{1,0:T(8,128)S(1)} %broadcast_subtract_fusion.slot_ref, bf16[16,16,256]{2,1,0:T(8,128)(2,1)S(1)} %collective-permute-done.2.left, bf16[16,16,256]{2,1,0:T(8,128)(2,1)S(1)} %get-tuple-element.50.own, bf16[16,16,256]{2,1,0:T(8,128)(2,1)S(1)} %collective-permute-done.3.right, ...), custom_call_target="tpu_custom_call" | custom-call | tf_op jit(solution)/shard_map/near/pallas_call | solution.py:179
  44.2 0.0 collective-permute-done.11.o3
  44.2 5.5 %down.1 = f32[4,4096]{1,0:T(4,128)} custom-call(s32[1,4096]{1,0:T(1,128)} %order.3, f32[4,8,256]{2,1,0:T(8,128)S(1)} %collective-permute-done.7.o1, f32[3,8,256]{2,1,0:T(8,128)S(1)} %collective-permute-done.8.q1, f32[2,8,256]{2,1,0:T(8,128)S(1)} %collective-permute-done.9.q2, f32[2,8,256]{2,1,0:T(8,128)S(1)} %collective-permute-done.10.q3, ...), custom_call_target="tpu_custom_call" | custom-call | tf_op jit(solution)/shard_map/down/pallas_call | solution.py:283
  (12 shorter events, 0.1 us)
Async XLA Ops:
  0.0 6.0 %copy-start = (bf16[1,4,2,16,256]{4,3,2,1,0:T(8,128)(2,1)S(1)}, bf16[1,4,2,16,256]{4,3,2,1,0:T(8,128)(2,1)}, u32[]{:S(2)}) copy-start(bf16[1,4,2,16,256]{4,3,2,1,0:T(8,128)(2,1)} %param.13) | copy-start | bytes 196612
  0.0 23.7 %copy-start.1 = (s32[16,8]{0,1:T(8,128)S(1)}, s32[16,8]{0,1:T(8,128)}, u32[]{:S(2)}) copy-start(s32[16,8]{0,1:T(8,128)} %param.10) | copy-start | bytes 1540
  0.0 6.0 %collective-permute-start = (bf16[8,16,256]{2,1,0:T(8,128)(2,1)}, bf16[8,16,256]{2,1,0:T(8,128)(2,1)S(1)}, u32[]{:S(2)}, u32[]{:S(2)}) collective-permute-start(bf16[8,16,256]{2,1,0:T(8,128)(2,1)} %bitcast.3), channel_id=1, source_target_pairs={{0,8},{1,9},{2,10},{3,11},{4,12},{5,13},{6,14},{7,15},{8,0},{9,1},... | collective-permute-start | bytes 196616 | tf_op jit(solution)/shard_map/ppermute | solution.py:198
  6.0 10.6 %collective-permute-start.1 = (bf16[2,8,16,256]{3,2,1,0:T(8,128)(2,1)S(1)}, bf16[2,8,16,256]{3,2,1,0:T(8,128)(2,1)S(1)}, u32[]{:S(2)}, u32[]{:S(2)}) collective-permute-start(bf16[2,8,16,256]{3,2,1,0:T(8,128)(2,1)S(1)} %pad_maximum_fusion.1), channel_id=1, source_target_pairs={{0,6},{1,7},{2,4},{3,5},{4,10},{5,11},{6,8},{7,9},{8,14},{9,15},{1... | collective-permute-start | bytes 393224 | tf_op jit(solution)/shard_map/ppermute | solution.py:198
  10.5 7.3 %collective-permute-start.3 = (bf16[16,16,256]{2,1,0:T(8,128)(2,1)S(1)}, bf16[16,16,256]{2,1,0:T(8,128)(2,1)S(1)}, u32[]{:S(2)}, u32[]{:S(2)}) collective-permute-start(bf16[16,16,256]{2,1,0:T(8,128)(2,1)S(1)} %get-tuple-element.50.own), channel_id=1, source_target_pairs={{0,240},{16,0},{32,16},{48,32},{64,48},{80,64},{96,80},{112,96},{1... | collective-permute-start | bytes 393224 | tf_op jit(solution)/shard_map/ppermute | solution.py:324
  15.2 5.6 %collective-permute-start.2 = (bf16[16,16,256]{2,1,0:T(8,128)(2,1)S(1)}, bf16[16,16,256]{2,1,0:T(8,128)(2,1)S(1)}, u32[]{:S(2)}, u32[]{:S(2)}) collective-permute-start(bf16[16,16,256]{2,1,0:T(8,128)(2,1)S(1)} %get-tuple-element.50.own), channel_id=1, source_target_pairs={{0,16},{16,32},{32,48},{48,64},{64,80},{80,96},{96,112},{112,128},... | collective-permute-start | bytes 393224 | tf_op jit(solution)/shard_map/ppermute | solution.py:323
  20.9 7.2 %collective-permute-start.6 = (bf16[4,7,16,256]{3,2,1,0:T(8,128)(2,1)S(1)}, bf16[4,7,16,256]{3,2,1,0:T(8,128)(2,1)S(1)}, u32[]{:S(2)}, u32[]{:S(2)}) collective-permute-start(bf16[4,7,16,256]{3,2,1,0:T(8,128)(2,1)S(1)} %fusion.5.refs_1_), channel_id=1, source_target_pairs={{0,4},{1,5},{2,6},{3,7},{4,8},{5,9},{6,10},{7,11},{8,12},{9,13},{1... | collective-permute-start | bytes 688136 | tf_op jit(solution)/shard_map/ppermute | solution.py:198
  21.7 6.6 %collective-permute-start.5 = (bf16[4,7,16,256]{3,2,1,0:T(8,128)(2,1)S(1)}, bf16[4,7,16,256]{3,2,1,0:T(8,128)(2,1)S(1)}, u32[]{:S(2)}, u32[]{:S(2)}) collective-permute-start(bf16[4,7,16,256]{3,2,1,0:T(8,128)(2,1)S(1)} %fusion.5.refs_1_), channel_id=1, source_target_pairs={{0,3},{1,0},{2,1},{3,2},{4,7},{5,4},{6,5},{7,6},{8,11},{9,8},{10,9... | collective-permute-start | bytes 688136 | tf_op jit(solution)/shard_map/ppermute | solution.py:198
  22.8 7.2 %collective-permute-start.4 = (bf16[4,7,16,256]{3,2,1,0:T(8,128)(2,1)S(1)}, bf16[4,7,16,256]{3,2,1,0:T(8,128)(2,1)S(1)}, u32[]{:S(2)}, u32[]{:S(2)}) collective-permute-start(bf16[4,7,16,256]{3,2,1,0:T(8,128)(2,1)S(1)} %fusion.5.refs_1_), channel_id=1, source_target_pairs={{0,1},{1,2},{2,3},{3,0},{4,5},{5,6},{6,7},{7,4},{8,9},{9,10},{10,1... | collective-permute-start | bytes 688136 | tf_op jit(solution)/shard_map/ppermute | solution.py:198
  30.6 1.4 %collective-permute-start.7 = (f32[4,8,256]{2,1,0:T(8,128)S(1)}, f32[4,8,256]{2,1,0:T(8,128)S(1)}, u32[]{:S(2)}, u32[]{:S(2)}) collective-permute-start(f32[4,8,256]{2,1,0:T(8,128)S(1)} %get-tuple-element.43), channel_id=1, source_target_pairs={{0,16},{16,0},{32,48},{48,32},{64,80},{80,64},{96,112},{112,96},{1... | collective-permute-start | bytes 98312 | tf_op jit(solution)/shard_map/ppermute | solution.py:302
  32.0 6.1 %collective-permute-start.8 = (f32[3,8,256]{2,1,0:T(8,128)S(1)}, f32[3,8,256]{2,1,0:T(8,128)S(1)}, u32[]{:S(2)}, u32[]{:S(2)}) collective-permute-start(f32[3,8,256]{2,1,0:T(8,128)S(1)} %slice_add_fusion), channel_id=1, source_target_pairs={{0,32},{16,48},{32,0},{48,16},{64,96},{80,112},{96,64},{112,80},{1... | collective-permute-start | bytes 73736 | tf_op jit(solution)/shard_map/ppermute | solution.py:302
  32.0 5.8 %collective-permute-start.10 = (f32[2,8,256]{2,1,0:T(8,128)S(1)}, f32[2,8,256]{2,1,0:T(8,128)S(1)}, u32[]{:S(2)}, u32[]{:S(2)}) collective-permute-start(f32[2,8,256]{2,1,0:T(8,128)S(1)} %slice.39), channel_id=1, source_target_pairs={{0,96},{16,112},{32,64},{48,80},{64,32},{80,48},{96,0},{112,16},{1... | collective-permute-start | bytes 49160 | tf_op jit(solution)/shard_map/ppermute | solution.py:302
  33.5 4.6 %collective-permute-start.9 = (f32[2,8,256]{2,1,0:T(8,128)S(1)}, f32[2,8,256]{2,1,0:T(8,128)S(1)}, u32[]{:S(2)}, u32[]{:S(2)}) collective-permute-start(f32[2,8,256]{2,1,0:T(8,128)S(1)} %slice.39), channel_id=1, source_target_pairs={{0,64},{16,80},{32,96},{48,112},{64,0},{80,16},{96,32},{112,48},{1... | collective-permute-start | bytes 49160 | tf_op jit(solution)/shard_map/ppermute | solution.py:302
  38.2 6.1 %collective-permute-start.11 = (f32[1,8,256]{2,1,0:T(8,128)S(1)}, f32[1,8,256]{2,1,0:T(8,128)S(1)}, u32[]{:S(2)}, u32[]{:S(2)}) collective-permute-start(f32[1,8,256]{2,1,0:T(8,128)S(1)} %fusion.7), channel_id=1, source_target_pairs={{0,192},{16,208},{32,224},{48,240},{64,128},{80,144},{96,160},{112... | collective-permute-start | bytes 24584 | tf_op jit(solution)/shard_map/ppermute | solution.py:302

commit v3 on v2

--- a/solution.py
+++ b/solution.py
@@ -163,7 +163,7 @@
     )(own)
 
 
-def near_kernel(first, count, slot_ref, left, own, right, base, pt, out, win):
+def near_leaves(first, count, slot_ref, left, own, right, base, pt, out, win):
     slots = slot_ref[...]
     win[0:16] = left[...]
     win[16:32] = own[...]
@@ -175,16 +175,60 @@
         out[l - first] = total
 
 
-def near(first, count, slots, left, own, right, base, pt):
+def near_kernel(first, count, *refs):
+    near_leaves(first, count, *refs)
+
+
+def near_fetch_kernel(
+    first, count, slots, left, own, right, base, pt, order, basis, lt, out, ov, bas, ev, ohs, win, sem
+):
+    copies, start = starter(sem)
+    start(order, ov)
+    for at in range(0, 30, 6):
+        start(lt.at[0, pl.ds(at, 6), 0], ev.at[pl.ds(at, 6)])
+    for at in range(0, 16, 4):
+        start(basis.at[pl.ds(at, 4)], bas.at[pl.ds(at, 4)])
+    copies[0].wait()
+    rows = lax.broadcasted_iota(jnp.int32, (256, 256), 0)
+    for t in range(16):
+        o = ov[:, t * 256 : t * 256 + 256]
+        ohs[t] = jnp.where(rows == (o & 255), 1.0, 0.0).astype(BF)
+    near_leaves(first, count, slots, left, own, right, base, pt, out, win)
+    for copy in copies[1:]:
+        copy.wait()
+
+
+WINDOW = pltpu.VMEM((48, 16, 256), BF)
+
+
+def near(first, count, parts):
     return pl.pallas_call(
         functools.partial(near_kernel, first, count),
         out_shape=jax.ShapeDtypeStruct((count, 8, 256), F32),
         in_specs=[VM] * 6,
         out_specs=VM,
-        scratch_shapes=[pltpu.VMEM((48, 16, 256), BF)],
+        scratch_shapes=[WINDOW],
         compiler_params=pltpu.CompilerParams(vmem_limit_bytes=8 * MB),
         name="near",
-    )(slots, left, own, right, base, pt)
+    )(*parts)
+
+
+def near_fetch(first, count, parts, order, basis, lt):
+    return pl.pallas_call(
+        functools.partial(near_fetch_kernel, first, count),
+        out_shape=(
+            jax.ShapeDtypeStruct((count, 8, 256), F32),
+            jax.ShapeDtypeStruct((1, 4096), jnp.int32),
+            jax.ShapeDtypeStruct((16, 256, 256), BF),
+            jax.ShapeDtypeStruct((30, 256, 256), BF),
+            jax.ShapeDtypeStruct((16, 256, 256), BF),
+        ),
+        in_specs=[VM] * 6 + [HBM] * 3,
+        out_specs=(VM,) * 5,
+        scratch_shapes=[WINDOW, pltpu.SemaphoreType.DMA((10,))],
+        compiler_params=pltpu.CompilerParams(vmem_limit_bytes=14 * MB),
+        name="near_fetch",
+    )(*parts, order, basis, lt)
 
 
 R1 = ((0, 0), (2, 0), (1, 2), (3, 2))
@@ -228,45 +272,21 @@
     )(root, *groups)
 
 
-def down_kernel(
-    order, o1, q1, q2, q3, o3, na, nb, nc, g, chain, basis, lt, out, ov, bas, ltv, f, ohs, sem
-):
-    copies, start = starter(sem)
-    start(order, ov)
-    start(lt.at[0, pl.ds(24, 6), 0], ltv.at[pl.ds(24, 6)])
-    start(lt.at[0, pl.ds(16, 8), 0], ltv.at[pl.ds(16, 8)])
-    for q in range(2):
-        start(lt.at[0, pl.ds(8 * q, 8), 0], ltv.at[pl.ds(8 * q, 8)])
-    for q in range(4):
-        start(basis.at[pl.ds(q * 4, 4)], bas.at[pl.ds(q * 4, 4)])
+def down_kernel(o1, q1, q2, q3, o3, na, nb, nc, g, chain, ov, bas, ev, ohs, out, f):
     top = o3[0]
     for term, k in ((q2[0] + q3[0], 2), (q1[0], 1), (o1[0], 0)):
         top = term + dot2(split(top), chain[2 * k], NT)
     f[0] = top
-    copies[0].wait()
-    rows = lax.broadcasted_iota(jnp.int32, (256, 256), 0)
-    for t in range(16):
-        o = ov[:, t * 256 : t * 256 + 256]
-        ohs[t] = jnp.where(rows == (o & 255), 1.0, 0.0).astype(BF)
     for start_slot, count in LEVELS[::-1]:
-        if start_slot == 28:
-            copies[1].wait()
-        if start_slot == 16:
-            copies[2].wait()
-        if start_slot == 0:
-            copies[3].wait()
-            copies[4].wait()
         for m in range(count // 2 - 1, -1, -1):
             slot = start_slot + 2 * m
             l = split(f[m])
-            f[2 * m + 1] = g[slot + 1] + dot2(l, ltv[slot + 1], NT)
-            f[2 * m] = g[slot] + dot2(l, ltv[slot], NT)
+            f[2 * m + 1] = g[slot + 1] + dot2(l, ev[slot + 1], NT)
+            f[2 * m] = g[slot] + dot2(l, ev[slot], NT)
     near_f = [r[i] for r in (na, nb, nc) for i in range(r.shape[0])]
     hrow = lax.broadcasted_iota(jnp.int32, (16, 256), 0)
     acc = jnp.zeros((128, 256), F32)
     for t in range(16):
-        if t % 4 == 0:
-            copies[5 + t // 4].wait()
         c = near_f[t] + dot2(split(f[t]), bas[t], NT)
         hit = hrow == (ov[:, t * 256 : t * 256 + 256] >> 8)
         ch = c.astype(BF).astype(F32)
@@ -279,23 +299,16 @@
             out[k : k + 1, h * 256 : h * 256 + 256] = both[h : h + 1]
 
 
-def down(order, parts, g, w, basis, lt):
+def down(parts, g, w, fetched):
     return pl.pallas_call(
         down_kernel,
         out_shape=jax.ShapeDtypeStruct((4, 4096), F32),
-        in_specs=[HBM] + [VM] * 10 + [HBM] * 2,
+        in_specs=[VM] * 14,
         out_specs=VM,
-        scratch_shapes=[
-            pltpu.VMEM((1, 4096), jnp.int32),
-            pltpu.VMEM((16, 256, 256), BF),
-            pltpu.VMEM((30, 256, 256), BF),
-            pltpu.VMEM((16, 8, 256), F32),
-            pltpu.VMEM((16, 256, 256), BF),
-            pltpu.SemaphoreType.DMA((9,)),
-        ],
-        compiler_params=pltpu.CompilerParams(vmem_limit_bytes=16 * MB),
+        scratch_shapes=[pltpu.VMEM((16, 8, 256), F32)],
+        compiler_params=pltpu.CompilerParams(vmem_limit_bytes=14 * MB),
         name="down",
-    )(order, *parts, g, w, basis, lt)
+    )(*parts, g, w, *fetched)
 
 
 def swapped(value, mask):
@@ -328,7 +341,8 @@
     row = jnp.concatenate([row[:, :6], row[:, 7:]], 1)
     groups = [row] + [shifted(row, s) for s in R2[1:]]
     slots = block_list - (lax.axis_index("leaf") * 16 - 16)
-    na = near(0, 8, slots, left, own, right, base, pt)
+    parts = (slots, left, own, right, base, pt)
+    na = near(0, 9, parts)
     *groups, na = tie(*groups, na)
     c, w = chain(root, groups)
     o1 = swapped(c, 1)
@@ -337,13 +351,15 @@
     q2 = swapped(s[1:], 4)
     q3 = swapped(s[1:], 6)
     own, _ = tie(own, s)
-    nb = near(8, 4, slots, left, own, right, base, pt)
+    parts = (slots, left, own, right, base, pt)
+    nb = near(9, 4, parts)
     q1, q2, q3, nb = tie(q1, q2, q3, nb)
     last = s[2:] + q1[2:] + q2[1:] + q3[1:]
     o3 = swapped(last, 12)
     own, _ = tie(own, last)
-    nc = near(12, 4, slots, left, own, right, base, pt)
-    return down(order, (o1, q1, q2, q3, o3, na, nb, nc), g, w, leaf_basis, local_transfers)
+    parts = (slots, left, own, right, base, pt)
+    nc, *fetched = near_fetch(13, 3, parts, order, leaf_basis, local_transfers)
+    return down((o1, q1, q2, q3, o3, na, nb, nc), g, w, fetched)
 
 
 def solution(mesh):

time: 50.1 us -> 49 us (0.978)
    pallas_call x0 -> x1, Pallas kernels: none -> 3.27 us  [near_fetch(): pl.pallas_call(functools.partial(near_fetch_kernel, first, count), out_sh...]
    pallas_call x1, Pallas kernels: 5.52 us -> 3.53 us  [down(): pl.pallas_call(down_kernel, out_shape=jax.ShapeDtypeStruct((4, 4096), F32...]
    pallas_call x3 -> x2, Pallas kernels: 8.93 us -> 7.17 us  [near(): pl.pallas_call(functools.partial(near_kernel, first, count), out_shape=ja...]
    ppermute x5, waiting for transfers between devices: 2.13 us -> 1.61 us  [shifted(): return lax.ppermute(value, 'probe', pairs)]
  transfers between devices with their start and end apart: 12 -> 12, of which waited for: 7 -> 7; matrix products, arithmetic and copies ran while one was open for 0% -> 0% of each run, Pallas kernels for 30% -> 33%
where the time goes in v3:
time: 49 us; the launch traced here: 48.8 us
  starting transfers between devices  20.7 us (42%)
  Pallas kernels  20.4 us (42%)
  waiting for transfers between devices  7.44 us (15%)
    ppermute x5, starting transfers between devices, shifted(): return lax.ppermute(value, 'probe', pairs)  8.51 us
    ppermute x5, starting transfers between devices, swapped(): return lax.ppermute(value, 'leaf', [(i, i ^ mask) for i in range(16)])  7.49 us
    pallas_call x2, Pallas kernels, near(): pl.pallas_call(functools.partial(near_kernel, first, count), out_shape=ja...  7.17 us
    ppermute x1, starting transfers between devices, shards(): right = lax.ppermute(own, 'leaf', [(i, (i - 1) % 16) for i in range(16)])  4.74 us
    pallas_call x1, Pallas kernels, up(): pl.pallas_call(up_kernel, out_shape=(jax.ShapeDtypeStruct((16, 16, 256),...  4.49 us
    pallas_call x1, Pallas kernels, down(): pl.pallas_call(down_kernel, out_shape=jax.ShapeDtypeStruct((4, 4096), F32...  3.53 us
    pallas_call x1, Pallas kernels, near_fetch(): pl.pallas_call(functools.partial(near_fetch_kernel, first, count), out_sh...  3.27 us
    ppermute x1, waiting for transfers between devices, shards(): left = lax.ppermute(own, 'leaf', [(i, (i + 1) % 16) for i in range(16)])  3.08 us
  transfers between devices with their start and end apart: 12, of which 7 were waited for; matrix products, arithmetic and copies ran while one was open for 0% of the time, Pallas kernels for 33%

profile of v3, /device:TPU:24, one launch (start us, length us, event | category | flops | bytes accessed | tf_op | source)
XLA Modules:
  0.0 48.8 jit_solution(5439415836380869555)
XLA Ops:
  0.0 1.2 %collective-permute-start = (bf16[8,16,256]{2,1,0:T(8,128)(2,1)}, bf16[8,16,256]{2,1,0:T(8,128)(2,1)S(1)}, u32[]{:S(2)}, u32[]{:S(2)}) collective-permute-start(bf16[8,16,256]{2,1,0:T(8,128)(2,1)} %bitcast.3), channel_id=1, source_target_pairs={{0,8},{1,9},{2,10},{3,11},{4,12},{5,13},{6,14},{7,15},{8,0},{9,1},... | collective-permute-start | bytes 196616 | tf_op jit(solution)/shard_map/ppermute | solution.py:242
  1.2 4.5 %up.1 = (bf16[16,16,256]{2,1,0:T(8,128)(2,1)S(1)}, f32[30,8,256]{2,1,0:T(8,128)S(1)}, f32[8,256]{1,0:T(8,128)S(1)}) custom-call(bf16[8,4096]{1,0:T(8,128)(2,1)} %points.1, bf16[4,4096]{1,0:T(4,128)(2,1)} %values.1, s32[1,4096]{1,0:T(1,128)} %order.3, bf16[16,256,256]{2,1,0:T(8,128)(2,1)} %basis.3, bf16[1,30,2,256,256]{4,3,2,1,0:T(8,128)(2,1)} %lt.3), custom_call_target="tpu_custom_call" | custom-call | tf_op jit(solution)/shard_map/up/pallas_call | solution.py:103
  5.7 0.2 collective-permute-done
  6.0 4.5 %collective-permute-start.1 = (bf16[2,8,16,256]{3,2,1,0:T(8,128)(2,1)S(1)}, bf16[2,8,16,256]{3,2,1,0:T(8,128)(2,1)S(1)}, u32[]{:S(2)}, u32[]{:S(2)}) collective-permute-start(bf16[2,8,16,256]{3,2,1,0:T(8,128)(2,1)S(1)} %pad_maximum_fusion.1), channel_id=1, source_target_pairs={{0,6},{1,7},{2,4},{3,5},{4,10},{5,11},{6,8},{7,9},{8,14},{9,15},{1... | collective-permute-start | bytes 393224 | tf_op jit(solution)/shard_map/ppermute | solution.py:242
  10.5 4.7 %collective-permute-start.3 = (bf16[16,16,256]{2,1,0:T(8,128)(2,1)S(1)}, bf16[16,16,256]{2,1,0:T(8,128)(2,1)S(1)}, u32[]{:S(2)}, u32[]{:S(2)}) collective-permute-start(bf16[16,16,256]{2,1,0:T(8,128)(2,1)S(1)} %get-tuple-element.55.own.refs_2_), channel_id=1, source_target_pairs={{0,240},{16,0},{32,16},{48,32},{64,48},{80,64},{96,80},{112,96},{1... | collective-permute-start | bytes 393224 | tf_op jit(solution)/shard_map/ppermute | solution.py:337
  15.2 0.0 collective-permute-start.2
  15.2 1.3 %near_own.1 = (f32[16,8,256]{2,1,0:T(8,128)S(1)}, bf16[16,256,16]{2,1,0:T(8,128)(2,1)S(1)}) custom-call(bf16[16,16,256]{2,1,0:T(8,128)(2,1)S(1)} %get-tuple-element.55.own.refs_2_), custom_call_target="tpu_custom_call" | custom-call | tf_op jit(solution)/shard_map/near_own/pallas_call | solution.py:153
  16.6 0.0 collective-permute-done.1
  16.6 1.2 %collective-permute-done.3.refs_3_.right = bf16[16,16,256]{2,1,0:T(8,128)(2,1)S(1)} collective-permute-done((bf16[16,16,256]{2,1,0:T(8,128)(2,1)S(1)}, bf16[16,16,256]{2,1,0:T(8,128)(2,1)S(1)}, u32[]{:S(2)}, u32[]{:S(2)}) %collective-permute-start.3) | collective-permute-done | bytes 131104 | tf_op jit(solution)/shard_map/ppermute | solution.py:337
  17.8 3.1 %collective-permute-done.2.refs_1_.left = bf16[16,16,256]{2,1,0:T(8,128)(2,1)S(1)} collective-permute-done((bf16[16,16,256]{2,1,0:T(8,128)(2,1)S(1)}, bf16[16,16,256]{2,1,0:T(8,128)(2,1)S(1)}, u32[]{:S(2)}, u32[]{:S(2)}) %collective-permute-start.2) | collective-permute-done | bytes 131104 | tf_op jit(solution)/shard_map/ppermute | solution.py:336
  20.9 0.8 %collective-permute-start.6 = (bf16[4,7,16,256]{3,2,1,0:T(8,128)(2,1)S(1)}, bf16[4,7,16,256]{3,2,1,0:T(8,128)(2,1)S(1)}, u32[]{:S(2)}, u32[]{:S(2)}) collective-permute-start(bf16[4,7,16,256]{3,2,1,0:T(8,128)(2,1)S(1)} %fusion.5.refs_1_), channel_id=1, source_target_pairs={{0,4},{1,5},{2,6},{3,7},{4,8},{5,9},{6,10},{7,11},{8,12},{9,13},{1... | collective-permute-start | bytes 688136 | tf_op jit(solution)/shard_map/ppermute | solution.py:242
  21.7 1.1 %collective-permute-start.5 = (bf16[4,7,16,256]{3,2,1,0:T(8,128)(2,1)S(1)}, bf16[4,7,16,256]{3,2,1,0:T(8,128)(2,1)S(1)}, u32[]{:S(2)}, u32[]{:S(2)}) collective-permute-start(bf16[4,7,16,256]{3,2,1,0:T(8,128)(2,1)S(1)} %fusion.5.refs_1_), channel_id=1, source_target_pairs={{0,3},{1,0},{2,1},{3,2},{4,7},{5,4},{6,5},{7,6},{8,11},{9,8},{10,9... | collective-permute-start | bytes 688136 | tf_op jit(solution)/shard_map/ppermute | solution.py:242
  22.8 0.9 %collective-permute-start.4 = (bf16[4,7,16,256]{3,2,1,0:T(8,128)(2,1)S(1)}, bf16[4,7,16,256]{3,2,1,0:T(8,128)(2,1)S(1)}, u32[]{:S(2)}, u32[]{:S(2)}) collective-permute-start(bf16[4,7,16,256]{3,2,1,0:T(8,128)(2,1)S(1)} %fusion.5.refs_1_), channel_id=1, source_target_pairs={{0,1},{1,2},{2,3},{3,0},{4,5},{5,6},{6,7},{7,4},{8,9},{9,10},{10,1... | collective-permute-start | bytes 688136 | tf_op jit(solution)/shard_map/ppermute | solution.py:242
  23.7 0.1 copy.8
  23.8 4.9 %near.2.na = f32[9,8,256]{2,1,0:T(8,128)S(1)} custom-call(s32[16,8]{1,0:T(8,128)S(1)} %broadcast_subtract_fusion.refs_0_.slots, bf16[16,16,256]{2,1,0:T(8,128)(2,1)S(1)} %collective-permute-done.2.refs_1_.left, bf16[16,16,256]{2,1,0:T(8,128)(2,1)S(1)} %get-tuple-element.55.own.refs_2_, bf16[16,16,256]{2,1,0:T(8,128)(2,1)S(1)} %collective-permute-done.3.refs_3_.right, ...), custom_call_target="tpu_custom_call" | custom-call | tf_op jit(solution)/shard_map/near/pallas_call | solution.py:205
  28.7 0.0 collective-permute-done.6.refs_4_
  28.7 0.1 collective-permute-done.5.refs_3_
  28.8 1.3 %collective-permute-done.4.refs_2_ = bf16[4,7,16,256]{3,2,1,0:T(8,128)(2,1)S(1)} collective-permute-done((bf16[4,7,16,256]{3,2,1,0:T(8,128)(2,1)S(1)}, bf16[4,7,16,256]{3,2,1,0:T(8,128)(2,1)S(1)}, u32[]{:S(2)}, u32[]{:S(2)}) %collective-permute-start.4) | collective-permute-done | bytes 229408 | tf_op jit(solution)/shard_map/ppermute | solution.py:242
  30.0 0.6 %chain.1 = (f32[4,8,256]{2,1,0:T(8,128)S(1)}, bf16[7,256,256]{2,1,0:T(8,128)(2,1)S(1)}) custom-call(f32[8,256]{1,0:T(8,128)S(1)} %get-tuple-element.34.refs_0_, bf16[4,7,16,256]{3,2,1,0:T(8,128)(2,1)S(1)} %fusion.5.refs_1_, bf16[4,7,16,256]{3,2,1,0:T(8,128)(2,1)S(1)} %collective-permute-done.4.refs_2_, ...), custom_call_target="tpu_custom_call" | custom-call | tf_op jit(solution)/shard_map/chain/pallas_call | solution.py:265
  30.6 0.0 collective-permute-start.7
  30.6 1.2 %collective-permute-done.7.o1 = f32[4,8,256]{2,1,0:T(8,128)S(1)} collective-permute-done((f32[4,8,256]{2,1,0:T(8,128)S(1)}, f32[4,8,256]{2,1,0:T(8,128)S(1)}, u32[]{:S(2)}, u32[]{:S(2)}) %collective-permute-start.7) | collective-permute-done | bytes 32800 | tf_op jit(solution)/shard_map/ppermute | solution.py:315
  31.9 0.0 collective-permute-start.8
  31.9 1.5 %collective-permute-start.10 = (f32[2,8,256]{2,1,0:T(8,128)S(1)}, f32[2,8,256]{2,1,0:T(8,128)S(1)}, u32[]{:S(2)}, u32[]{:S(2)}) collective-permute-start(f32[2,8,256]{2,1,0:T(8,128)S(1)} %slice.39), channel_id=1, source_target_pairs={{0,96},{16,112},{32,64},{48,80},{64,32},{80,48},{96,0},{112,16},{1... | collective-permute-start | bytes 49160 | tf_op jit(solution)/shard_map/ppermute | solution.py:315
  33.4 2.0 %collective-permute-start.9 = (f32[2,8,256]{2,1,0:T(8,128)S(1)}, f32[2,8,256]{2,1,0:T(8,128)S(1)}, u32[]{:S(2)}, u32[]{:S(2)}) collective-permute-start(f32[2,8,256]{2,1,0:T(8,128)S(1)} %slice.39), channel_id=1, source_target_pairs={{0,64},{16,80},{32,96},{48,112},{64,0},{80,16},{96,32},{112,48},{1... | collective-permute-start | bytes 49160 | tf_op jit(solution)/shard_map/ppermute | solution.py:315
  35.4 2.3 %near.3.nb = f32[4,8,256]{2,1,0:T(8,128)S(1)} custom-call(s32[16,8]{1,0:T(8,128)S(1)} %broadcast_subtract_fusion.refs_0_.slots, bf16[16,16,256]{2,1,0:T(8,128)(2,1)S(1)} %collective-permute-done.2.refs_1_.left, bf16[16,16,256]{2,1,0:T(8,128)(2,1)S(1)} %get-tuple-element.55.own.refs_2_, bf16[16,16,256]{2,1,0:T(8,128)(2,1)S(1)} %collective-permute-done.3.refs_3_.right, ...), custom_call_target="tpu_custom_call" | custom-call | tf_op jit(solution)/shard_map/near/pallas_call | solution.py:205
  37.6 0.0 collective-permute-done.10.q3
  37.6 0.3 collective-permute-done.9.q2
  38.0 0.0 collective-permute-done.8.q1
  38.0 4.0 %collective-permute-start.11 = (f32[1,8,256]{2,1,0:T(8,128)S(1)}, f32[1,8,256]{2,1,0:T(8,128)S(1)}, u32[]{:S(2)}, u32[]{:S(2)}) collective-permute-start(f32[1,8,256]{2,1,0:T(8,128)S(1)} %fusion.7), channel_id=1, source_target_pairs={{0,192},{16,208},{32,224},{48,240},{64,128},{80,144},{96,160},{112... | collective-permute-start | bytes 24584 | tf_op jit(solution)/shard_map/ppermute | solution.py:315
  42.0 3.3 %near_fetch.1 = (f32[3,8,256]{2,1,0:T(8,128)S(1)}, s32[1,4096]{1,0:T(1,128)S(1)}, bf16[16,256,256]{2,1,0:T(8,128)(2,1)S(1)}, bf16[30,256,256]{2,1,0:T(8,128)(2,1)S(1)}, bf16[16,256,256]{2,1,0:T(8,128)(2,1)S(1)}) custom-call(s32[16,8]{1,0:T(8,128)S(1)} %broadcast_subtract_fusion.refs_0_.slots, bf16[16,16,256]{2,1,0:T(8,128)(2,1)S(1)} %collective-permute-done.2.refs_1_.left, ...), custom_call_target="tpu_custom_call" | custom-call | tf_op jit(solution)/shard_map/near_fetch/pallas_call | solution.py:217
  45.3 0.0 collective-permute-done.11.o3
  45.3 3.5 %down.1 = f32[4,4096]{1,0:T(4,128)} custom-call(f32[4,8,256]{2,1,0:T(8,128)S(1)} %collective-permute-done.7.o1, f32[3,8,256]{2,1,0:T(8,128)S(1)} %collective-permute-done.8.q1, f32[2,8,256]{2,1,0:T(8,128)S(1)} %collective-permute-done.9.q2, f32[2,8,256]{2,1,0:T(8,128)S(1)} %collective-permute-done.10.q3, f32[1,8,256]{2,1,0:T(8,128)S(1)} %collective-permute-done.11.o3, ...), custom_call_target="tpu_custom_call" | custom-call | tf_op jit(solution)/shard_map/down/pallas_call | solution.py:303
  (12 shorter events, 0.1 us)
Async XLA Ops:
  0.0 6.0 %copy-start = (bf16[1,4,2,16,256]{4,3,2,1,0:T(8,128)(2,1)S(1)}, bf16[1,4,2,16,256]{4,3,2,1,0:T(8,128)(2,1)}, u32[]{:S(2)}) copy-start(bf16[1,4,2,16,256]{4,3,2,1,0:T(8,128)(2,1)} %param.13) | copy-start | bytes 196612
  0.0 23.7 %copy-start.1 = (s32[16,8]{0,1:T(8,128)S(1)}, s32[16,8]{0,1:T(8,128)}, u32[]{:S(2)}) copy-start(s32[16,8]{0,1:T(8,128)} %param.10) | copy-start | bytes 1540
  0.0 6.0 %collective-permute-start = (bf16[8,16,256]{2,1,0:T(8,128)(2,1)}, bf16[8,16,256]{2,1,0:T(8,128)(2,1)S(1)}, u32[]{:S(2)}, u32[]{:S(2)}) collective-permute-start(bf16[8,16,256]{2,1,0:T(8,128)(2,1)} %bitcast.3), channel_id=1, source_target_pairs={{0,8},{1,9},{2,10},{3,11},{4,12},{5,13},{6,14},{7,15},{8,0},{9,1},... | collective-permute-start | bytes 196616 | tf_op jit(solution)/shard_map/ppermute | solution.py:242
  6.0 10.6 %collective-permute-start.1 = (bf16[2,8,16,256]{3,2,1,0:T(8,128)(2,1)S(1)}, bf16[2,8,16,256]{3,2,1,0:T(8,128)(2,1)S(1)}, u32[]{:S(2)}, u32[]{:S(2)}) collective-permute-start(bf16[2,8,16,256]{3,2,1,0:T(8,128)(2,1)S(1)} %pad_maximum_fusion.1), channel_id=1, source_target_pairs={{0,6},{1,7},{2,4},{3,5},{4,10},{5,11},{6,8},{7,9},{8,14},{9,15},{1... | collective-permute-start | bytes 393224 | tf_op jit(solution)/shard_map/ppermute | solution.py:242
  10.5 7.3 %collective-permute-start.3 = (bf16[16,16,256]{2,1,0:T(8,128)(2,1)S(1)}, bf16[16,16,256]{2,1,0:T(8,128)(2,1)S(1)}, u32[]{:S(2)}, u32[]{:S(2)}) collective-permute-start(bf16[16,16,256]{2,1,0:T(8,128)(2,1)S(1)} %get-tuple-element.55.own.refs_2_), channel_id=1, source_target_pairs={{0,240},{16,0},{32,16},{48,32},{64,48},{80,64},{96,80},{112,96},{1... | collective-permute-start | bytes 393224 | tf_op jit(solution)/shard_map/ppermute | solution.py:337
  15.2 5.6 %collective-permute-start.2 = (bf16[16,16,256]{2,1,0:T(8,128)(2,1)S(1)}, bf16[16,16,256]{2,1,0:T(8,128)(2,1)S(1)}, u32[]{:S(2)}, u32[]{:S(2)}) collective-permute-start(bf16[16,16,256]{2,1,0:T(8,128)(2,1)S(1)} %get-tuple-element.55.own.refs_2_), channel_id=1, source_target_pairs={{0,16},{16,32},{32,48},{48,64},{64,80},{80,96},{96,112},{112,128},... | collective-permute-start | bytes 393224 | tf_op jit(solution)/shard_map/ppermute | solution.py:336
  20.9 7.8 %collective-permute-start.6 = (bf16[4,7,16,256]{3,2,1,0:T(8,128)(2,1)S(1)}, bf16[4,7,16,256]{3,2,1,0:T(8,128)(2,1)S(1)}, u32[]{:S(2)}, u32[]{:S(2)}) collective-permute-start(bf16[4,7,16,256]{3,2,1,0:T(8,128)(2,1)S(1)} %fusion.5.refs_1_), channel_id=1, source_target_pairs={{0,4},{1,5},{2,6},{3,7},{4,8},{5,9},{6,10},{7,11},{8,12},{9,13},{1... | collective-permute-start | bytes 688136 | tf_op jit(solution)/shard_map/ppermute | solution.py:242
  21.7 7.1 %collective-permute-start.5 = (bf16[4,7,16,256]{3,2,1,0:T(8,128)(2,1)S(1)}, bf16[4,7,16,256]{3,2,1,0:T(8,128)(2,1)S(1)}, u32[]{:S(2)}, u32[]{:S(2)}) collective-permute-start(bf16[4,7,16,256]{3,2,1,0:T(8,128)(2,1)S(1)} %fusion.5.refs_1_), channel_id=1, source_target_pairs={{0,3},{1,0},{2,1},{3,2},{4,7},{5,4},{6,5},{7,6},{8,11},{9,8},{10,9... | collective-permute-start | bytes 688136 | tf_op jit(solution)/shard_map/ppermute | solution.py:242
  22.8 7.2 %collective-permute-start.4 = (bf16[4,7,16,256]{3,2,1,0:T(8,128)(2,1)S(1)}, bf16[4,7,16,256]{3,2,1,0:T(8,128)(2,1)S(1)}, u32[]{:S(2)}, u32[]{:S(2)}) collective-permute-start(bf16[4,7,16,256]{3,2,1,0:T(8,128)(2,1)S(1)} %fusion.5.refs_1_), channel_id=1, source_target_pairs={{0,1},{1,2},{2,3},{3,0},{4,5},{5,6},{6,7},{7,4},{8,9},{9,10},{10,1... | collective-permute-start | bytes 688136 | tf_op jit(solution)/shard_map/ppermute | solution.py:242
  30.6 1.2 %collective-permute-start.7 = (f32[4,8,256]{2,1,0:T(8,128)S(1)}, f32[4,8,256]{2,1,0:T(8,128)S(1)}, u32[]{:S(2)}, u32[]{:S(2)}) collective-permute-start(f32[4,8,256]{2,1,0:T(8,128)S(1)} %get-tuple-element.48), channel_id=1, source_target_pairs={{0,16},{16,0},{32,48},{48,32},{64,80},{80,64},{96,112},{112,96},{1... | collective-permute-start | bytes 98312 | tf_op jit(solution)/shard_map/ppermute | solution.py:315
  31.9 6.1 %collective-permute-start.8 = (f32[3,8,256]{2,1,0:T(8,128)S(1)}, f32[3,8,256]{2,1,0:T(8,128)S(1)}, u32[]{:S(2)}, u32[]{:S(2)}) collective-permute-start(f32[3,8,256]{2,1,0:T(8,128)S(1)} %slice_add_fusion), channel_id=1, source_target_pairs={{0,32},{16,48},{32,0},{48,16},{64,96},{80,112},{96,64},{112,80},{1... | collective-permute-start | bytes 73736 | tf_op jit(solution)/shard_map/ppermute | solution.py:315
  31.9 5.8 %collective-permute-start.10 = (f32[2,8,256]{2,1,0:T(8,128)S(1)}, f32[2,8,256]{2,1,0:T(8,128)S(1)}, u32[]{:S(2)}, u32[]{:S(2)}) collective-permute-start(f32[2,8,256]{2,1,0:T(8,128)S(1)} %slice.39), channel_id=1, source_target_pairs={{0,96},{16,112},{32,64},{48,80},{64,32},{80,48},{96,0},{112,16},{1... | collective-permute-start | bytes 49160 | tf_op jit(solution)/shard_map/ppermute | solution.py:315
  33.4 4.6 %collective-permute-start.9 = (f32[2,8,256]{2,1,0:T(8,128)S(1)}, f32[2,8,256]{2,1,0:T(8,128)S(1)}, u32[]{:S(2)}, u32[]{:S(2)}) collective-permute-start(f32[2,8,256]{2,1,0:T(8,128)S(1)} %slice.39), channel_id=1, source_target_pairs={{0,64},{16,80},{32,96},{48,112},{64,0},{80,16},{96,32},{112,48},{1... | collective-permute-start | bytes 49160 | tf_op jit(solution)/shard_map/ppermute | solution.py:315
  38.0 7.3 %collective-permute-start.11 = (f32[1,8,256]{2,1,0:T(8,128)S(1)}, f32[1,8,256]{2,1,0:T(8,128)S(1)}, u32[]{:S(2)}, u32[]{:S(2)}) collective-permute-start(f32[1,8,256]{2,1,0:T(8,128)S(1)} %fusion.7), channel_id=1, source_target_pairs={{0,192},{16,208},{32,224},{48,240},{64,128},{80,144},{96,160},{112... | collective-permute-start | bytes 24584 | tf_op jit(solution)/shard_map/ppermute | solution.py:315

commit v4 on v3

--- a/solution.py
+++ b/solution.py
@@ -44,7 +44,7 @@
     return copies, start
 
 
-def up_kernel(points, values, order, basis, lt, td, g, root, pv, vv, ov, xs, xr, bas, ltv, s, sem):
+def up_kernel(points, values, order, basis, lt, td, s0, g, root, pv, vv, ov, xs, xr, bas, ltv, s, sem):
     copies, start = starter(sem)
     start(points, pv)
     start(values, vv)
@@ -52,7 +52,7 @@
     for q in range(2):
         start(basis.at[pl.ds(q * 8, 8)], bas.at[pl.ds(q * 8, 8)])
     for q in range(4):
-        start(lt.at[0, pl.ds(q * 4, 4)], ltv.at[pl.ds(q * 4, 4)])
+        start(lt.at[0, pl.ds(q * 4, 4), 0], ltv.at[pl.ds(q * 4, 4), 0])
     for q in range(2):
         start(lt.at[0, pl.ds(16 + q * 4, 4)], ltv.at[pl.ds(16 + q * 4, 4)])
     start(lt.at[0, pl.ds(24, 6)], ltv.at[pl.ds(24, 6)])
@@ -83,7 +83,7 @@
         if l % 8 == 0:
             copies[3 + l // 8].wait()
         r = dot(td[l], bas[l])
-        s[l] = jnp.where(sub < 4, r[8:], 0.0)
+        s0[l] = jnp.where(sub < 4, r[8:], 0.0)
     for start_slot, count in LEVELS:
         for n in range(0, count, 2):
             slot = start_slot + n
@@ -91,10 +91,12 @@
                 copies[5 + slot // 4].wait()
             if slot == 24:
                 copies[11].wait()
-            l0 = split(s[n])
-            l1 = split(s[n + 1])
-            g[slot + 1] = dot2(l0, ltv[slot, 1])
-            g[slot] = dot2(l1, ltv[slot + 1, 1])
+            level = s if start_slot else s0
+            l0 = split(level[n])
+            l1 = split(level[n + 1])
+            if start_slot:
+                g[slot - 15] = dot2(l0, ltv[slot, 1])
+                g[slot - 16] = dot2(l1, ltv[slot + 1, 1])
             s[n // 2] = dot2(l0, ltv[slot, 0]) + dot2(l1, ltv[slot + 1, 0])
     root[...] = s[0]
 
@@ -104,11 +106,12 @@
         up_kernel,
         out_shape=(
             jax.ShapeDtypeStruct((16, 16, 256), BF),
-            jax.ShapeDtypeStruct((30, 8, 256), F32),
+            jax.ShapeDtypeStruct((16, 8, 256), F32),
+            jax.ShapeDtypeStruct((14, 8, 256), F32),
             jax.ShapeDtypeStruct((8, 256), F32),
         ),
         in_specs=[HBM] * 5,
-        out_specs=(VM, VM, VM),
+        out_specs=(VM,) * 4,
         scratch_shapes=[
             pltpu.VMEM((8, 4096), BF),
             pltpu.VMEM((4, 4096), BF),
@@ -143,24 +146,33 @@
     return dot(q, pltpu.reciprocal(f * f * f, approx=True).astype(BF), NT)[8:]
 
 
-def near_own_kernel(own, out, pt):
+def near_own_kernel(own, s0, lt, out, pt, g, cv, sem):
+    copies, start = starter(sem)
+    for q in range(2):
+        start(lt.at[0, pl.ds(q * 8, 8), 1], cv.at[pl.ds(q * 8, 8)])
     for l in range(16):
         pt[l] = sources(own.at[l])
         out[l] = block(pt[l], own[l])
-
-
-def near_own(own):
+    for l in range(16):
+        if l % 8 == 0:
+            copies[l // 8].wait()
+        g[l ^ 1] = dot2(split(s0[l]), cv[l])
+
+
+def near_own(own, s0, lt):
     return pl.pallas_call(
         near_own_kernel,
         out_shape=(
             jax.ShapeDtypeStruct((16, 8, 256), F32),
             jax.ShapeDtypeStruct((16, 256, 16), BF),
+            jax.ShapeDtypeStruct((16, 8, 256), F32),
         ),
-        in_specs=[VM],
-        out_specs=(VM, VM),
-        compiler_params=pltpu.CompilerParams(vmem_limit_bytes=4 * MB),
+        in_specs=[VM, VM, HBM],
+        out_specs=(VM,) * 3,
+        scratch_shapes=[pltpu.VMEM((16, 256, 256), BF), pltpu.SemaphoreType.DMA((2,))],
+        compiler_params=pltpu.CompilerParams(vmem_limit_bytes=6 * MB),
         name="near_own",
-    )(own)
+    )(own, s0, lt)
 
 
 def near_leaves(first, count, slot_ref, left, own, right, base, pt, out, win):
@@ -184,10 +196,9 @@
 ):
     copies, start = starter(sem)
     start(order, ov)
-    for at in range(0, 30, 6):
-        start(lt.at[0, pl.ds(at, 6), 0], ev.at[pl.ds(at, 6)])
-    for at in range(0, 16, 4):
-        start(basis.at[pl.ds(at, 4)], bas.at[pl.ds(at, 4)])
+    for at in range(0, 30, 15):
+        start(lt.at[0, pl.ds(at, 15), 0], ev.at[pl.ds(at, 15)])
+    start(basis, bas)
     copies[0].wait()
     rows = lax.broadcasted_iota(jnp.int32, (256, 256), 0)
     for t in range(16):
@@ -225,7 +236,7 @@
         ),
         in_specs=[VM] * 6 + [HBM] * 3,
         out_specs=(VM,) * 5,
-        scratch_shapes=[WINDOW, pltpu.SemaphoreType.DMA((10,))],
+        scratch_shapes=[WINDOW, pltpu.SemaphoreType.DMA((4,))],
         compiler_params=pltpu.CompilerParams(vmem_limit_bytes=14 * MB),
         name="near_fetch",
     )(*parts, order, basis, lt)
@@ -272,7 +283,8 @@
     )(root, *groups)
 
 
-def down_kernel(o1, q1, q2, q3, o3, na, nb, nc, g, chain, ov, bas, ev, ohs, out, f):
+def down_kernel(o1, q1, q2, q3, o3, na, nb, nc, g0, g1, chain, ov, bas, ev, ohs, out, f):
+    g = [g0[i] for i in range(16)] + [g1[i] for i in range(14)]
     top = o3[0]
     for term, k in ((q2[0] + q3[0], 2), (q1[0], 1), (o1[0], 0)):
         top = term + dot2(split(top), chain[2 * k], NT)
@@ -299,16 +311,16 @@
             out[k : k + 1, h * 256 : h * 256 + 256] = both[h : h + 1]
 
 
-def down(parts, g, w, fetched):
+def down(parts, g0, g1, w, fetched):
     return pl.pallas_call(
         down_kernel,
         out_shape=jax.ShapeDtypeStruct((4, 4096), F32),
-        in_specs=[VM] * 14,
+        in_specs=[VM] * 15,
         out_specs=VM,
         scratch_shapes=[pltpu.VMEM((16, 8, 256), F32)],
         compiler_params=pltpu.CompilerParams(vmem_limit_bytes=14 * MB),
         name="down",
-    )(*parts, g, w, *fetched)
+    )(*parts, g0, g1, w, *fetched)
 
 
 def swapped(value, mask):
@@ -329,13 +341,13 @@
     )
     shard = chain_transfers.reshape(8, 16, 256)
     pair = shifted(shard, R1[1])
-    own, g, root = up(points, values, order, leaf_basis, local_transfers)
+    own, s0, g, root = up(points, values, order, leaf_basis, local_transfers)
     pair, own = tie(pair, own)
     pair = jnp.stack([shard, pair])
     other = shifted(pair, R1[2])
     left = lax.ppermute(own, "leaf", [(i, (i + 1) % 16) for i in range(16)])
     right = lax.ppermute(own, "leaf", [(i, (i - 1) % 16) for i in range(16)])
-    base, pt = near_own(own)
+    base, pt, g0 = near_own(own, s0, local_transfers)
     other, base, left, right = tie(other, base, left, right)
     row = jnp.concatenate([pair, other], 0)
     row = jnp.concatenate([row[:, :6], row[:, 7:]], 1)
@@ -359,7 +371,7 @@
     own, _ = tie(own, last)
     parts = (slots, left, own, right, base, pt)
     nc, *fetched = near_fetch(13, 3, parts, order, leaf_basis, local_transfers)
-    return down((o1, q1, q2, q3, o3, na, nb, nc), g, w, fetched)
+    return down((o1, q1, q2, q3, o3, na, nb, nc), g0, g, w, fetched)
 
 
 def solution(mesh):

time: 49 us -> 48.7 us (level)
  waiting for transfers between devices: 7.44 us -> 6.54 us
  Pallas kernels: 20.4 us -> 21.2 us
    ppermute x1, waiting for transfers between devices: 1.18 us -> 0.01 us  [shards(): right = lax.ppermute(own, 'leaf', [(i, (i - 1) % 16) for i in range(16)])]
    pallas_call x1, Pallas kernels: 1.33 us -> 2.5 us  [near_own(): pl.pallas_call(near_own_kernel, out_shape=(jax.ShapeDtypeStruct((16, 8, 2...]
  transfers between devices with their start and end apart: 12 -> 12, of which waited for: 7 -> 6; matrix products, arithmetic and copies ran while one was open for 0% -> 0% of each run, Pallas kernels for 33% -> 35%
where the time goes in v4:
time: 48.7 us; the launch traced here: 48.5 us
  Pallas kernels  21.2 us (44%)
  starting transfers between devices  20.5 us (42%)
  waiting for transfers between devices  6.54 us (13%)
    ppermute x5, starting transfers between devices, shifted(): return lax.ppermute(value, 'probe', pairs)  8.24 us
    ppermute x5, starting transfers between devices, swapped(): return lax.ppermute(value, 'leaf', [(i, i ^ mask) for i in range(16)])  7.48 us
    pallas_call x2, Pallas kernels, near(): pl.pallas_call(functools.partial(near_kernel, first, count), out_shape=ja...  7.17 us
    ppermute x1, starting transfers between devices, shards(): right = lax.ppermute(own, 'leaf', [(i, (i - 1) % 16) for i in range(16)])  4.74 us
    pallas_call x1, Pallas kernels, up(): pl.pallas_call(up_kernel, out_shape=(jax.ShapeDtypeStruct((16, 16, 256),...  4.21 us
    pallas_call x1, Pallas kernels, down(): pl.pallas_call(down_kernel, out_shape=jax.ShapeDtypeStruct((4, 4096), F32...  3.54 us
    pallas_call x1, Pallas kernels, near_fetch(): pl.pallas_call(functools.partial(near_fetch_kernel, first, count), out_sh...  3.21 us
    ppermute x1, waiting for transfers between devices, shards(): left = lax.ppermute(own, 'leaf', [(i, (i + 1) % 16) for i in range(16)])  3.07 us
  transfers between devices with their start and end apart: 12, of which 6 were waited for; matrix products, arithmetic and copies ran while one was open for 0% of the time, Pallas kernels for 35%

profile of v4, /device:TPU:24, one launch (start us, length us, event | category | flops | bytes accessed | tf_op | source)
XLA Modules:
  0.0 48.5 jit_solution(2454369697311363812)
XLA Ops:
  0.0 1.2 %collective-permute-start = (bf16[8,16,256]{2,1,0:T(8,128)(2,1)}, bf16[8,16,256]{2,1,0:T(8,128)(2,1)S(1)}, u32[]{:S(2)}, u32[]{:S(2)}) collective-permute-start(bf16[8,16,256]{2,1,0:T(8,128)(2,1)} %bitcast.3), channel_id=1, source_target_pairs={{0,8},{1,9},{2,10},{3,11},{4,12},{5,13},{6,14},{7,15},{8,0},{9,1},... | collective-permute-start | bytes 196616 | tf_op jit(solution)/shard_map/ppermute | solution.py:253
  1.2 4.2 %up.1 = (bf16[16,16,256]{2,1,0:T(8,128)(2,1)S(1)}, f32[16,8,256]{2,1,0:T(8,128)S(1)}, f32[14,8,256]{2,1,0:T(8,128)S(1)}, f32[8,256]{1,0:T(8,128)S(1)}) custom-call(bf16[8,4096]{1,0:T(8,128)(2,1)} %points.1, bf16[4,4096]{1,0:T(4,128)(2,1)} %values.1, s32[1,4096]{1,0:T(1,128)} %order.3, bf16[16,256,256]{2,1,0:T(8,128)(2,1)} %basis.3, ...), custom_call_target="tpu_custom_call" | custom-call | tf_op jit(solution)/shard_map/up/pallas_call | solution.py:105
  5.5 0.5 %collective-permute-done = bf16[8,16,256]{2,1,0:T(8,128)(2,1)S(1)} collective-permute-done((bf16[8,16,256]{2,1,0:T(8,128)(2,1)}, bf16[8,16,256]{2,1,0:T(8,128)(2,1)S(1)}, u32[]{:S(2)}, u32[]{:S(2)}) %collective-permute-start) | collective-permute-done | bytes 65568 | tf_op jit(solution)/shard_map/ppermute | solution.py:253
  6.0 4.2 %collective-permute-start.1 = (bf16[2,8,16,256]{3,2,1,0:T(8,128)(2,1)S(1)}, bf16[2,8,16,256]{3,2,1,0:T(8,128)(2,1)S(1)}, u32[]{:S(2)}, u32[]{:S(2)}) collective-permute-start(bf16[2,8,16,256]{3,2,1,0:T(8,128)(2,1)S(1)} %pad_maximum_fusion.1), channel_id=1, source_target_pairs={{0,6},{1,7},{2,4},{3,5},{4,10},{5,11},{6,8},{7,9},{8,14},{9,15},{1... | collective-permute-start | bytes 393224 | tf_op jit(solution)/shard_map/ppermute | solution.py:253
  10.2 4.7 %collective-permute-start.3 = (bf16[16,16,256]{2,1,0:T(8,128)(2,1)S(1)}, bf16[16,16,256]{2,1,0:T(8,128)(2,1)S(1)}, u32[]{:S(2)}, u32[]{:S(2)}) collective-permute-start(bf16[16,16,256]{2,1,0:T(8,128)(2,1)S(1)} %get-tuple-element.58.own.refs_2_), channel_id=1, source_target_pairs={{0,240},{16,0},{32,16},{48,32},{64,48},{80,64},{96,80},{112,96},{1... | collective-permute-start | bytes 393224 | tf_op jit(solution)/shard_map/ppermute | solution.py:349
  15.0 0.0 collective-permute-start.2
  15.0 2.5 %near_own.1 = (f32[16,8,256]{2,1,0:T(8,128)S(1)}, bf16[16,256,16]{2,1,0:T(8,128)(2,1)S(1)}, f32[16,8,256]{2,1,0:T(8,128)S(1)}) custom-call(bf16[16,16,256]{2,1,0:T(8,128)(2,1)S(1)} %get-tuple-element.58.own.refs_2_, f32[16,8,256]{2,1,0:T(8,128)S(1)} %get-tuple-element.40.s0, bf16[1,30,2,256,256]{4,3,2,1,0:T(8,128)(2,1)} %lt.5), custom_call_target="tpu_custom_call" | custom-call | tf_op jit(solution)/shard_map/near_own/pallas_call | solution.py:163
  17.5 0.0 collective-permute-done.1
  17.5 0.0 collective-permute-done.3.refs_3_.right
  17.5 3.1 %collective-permute-done.2.refs_1_.left = bf16[16,16,256]{2,1,0:T(8,128)(2,1)S(1)} collective-permute-done((bf16[16,16,256]{2,1,0:T(8,128)(2,1)S(1)}, bf16[16,16,256]{2,1,0:T(8,128)(2,1)S(1)}, u32[]{:S(2)}, u32[]{:S(2)}) %collective-permute-start.2) | collective-permute-done | bytes 131104 | tf_op jit(solution)/shard_map/ppermute | solution.py:348
  20.7 0.8 %collective-permute-start.6 = (bf16[4,7,16,256]{3,2,1,0:T(8,128)(2,1)S(1)}, bf16[4,7,16,256]{3,2,1,0:T(8,128)(2,1)S(1)}, u32[]{:S(2)}, u32[]{:S(2)}) collective-permute-start(bf16[4,7,16,256]{3,2,1,0:T(8,128)(2,1)S(1)} %fusion.5.refs_1_), channel_id=1, source_target_pairs={{0,4},{1,5},{2,6},{3,7},{4,8},{5,9},{6,10},{7,11},{8,12},{9,13},{1... | collective-permute-start | bytes 688136 | tf_op jit(solution)/shard_map/ppermute | solution.py:253
  21.4 1.1 %collective-permute-start.5 = (bf16[4,7,16,256]{3,2,1,0:T(8,128)(2,1)S(1)}, bf16[4,7,16,256]{3,2,1,0:T(8,128)(2,1)S(1)}, u32[]{:S(2)}, u32[]{:S(2)}) collective-permute-start(bf16[4,7,16,256]{3,2,1,0:T(8,128)(2,1)S(1)} %fusion.5.refs_1_), channel_id=1, source_target_pairs={{0,3},{1,0},{2,1},{3,2},{4,7},{5,4},{6,5},{7,6},{8,11},{9,8},{10,9... | collective-permute-start | bytes 688136 | tf_op jit(solution)/shard_map/ppermute | solution.py:253
  22.5 0.9 %collective-permute-start.4 = (bf16[4,7,16,256]{3,2,1,0:T(8,128)(2,1)S(1)}, bf16[4,7,16,256]{3,2,1,0:T(8,128)(2,1)S(1)}, u32[]{:S(2)}, u32[]{:S(2)}) collective-permute-start(bf16[4,7,16,256]{3,2,1,0:T(8,128)(2,1)S(1)} %fusion.5.refs_1_), channel_id=1, source_target_pairs={{0,1},{1,2},{2,3},{3,0},{4,5},{5,6},{6,7},{7,4},{8,9},{9,10},{10,1... | collective-permute-start | bytes 688136 | tf_op jit(solution)/shard_map/ppermute | solution.py:253
  23.4 0.1 copy.8
  23.5 4.9 %near.2.na = f32[9,8,256]{2,1,0:T(8,128)S(1)} custom-call(s32[16,8]{1,0:T(8,128)S(1)} %broadcast_subtract_fusion.refs_0_.slots, bf16[16,16,256]{2,1,0:T(8,128)(2,1)S(1)} %collective-permute-done.2.refs_1_.left, bf16[16,16,256]{2,1,0:T(8,128)(2,1)S(1)} %get-tuple-element.58.own.refs_2_, bf16[16,16,256]{2,1,0:T(8,128)(2,1)S(1)} %collective-permute-done.3.refs_3_.right, ...), custom_call_target="tpu_custom_call" | custom-call | tf_op jit(solution)/shard_map/near/pallas_call | solution.py:216
  28.4 0.0 collective-permute-done.6.refs_4_
  28.4 0.1 collective-permute-done.5.refs_3_
  28.5 1.2 %collective-permute-done.4.refs_2_ = bf16[4,7,16,256]{3,2,1,0:T(8,128)(2,1)S(1)} collective-permute-done((bf16[4,7,16,256]{3,2,1,0:T(8,128)(2,1)S(1)}, bf16[4,7,16,256]{3,2,1,0:T(8,128)(2,1)S(1)}, u32[]{:S(2)}, u32[]{:S(2)}) %collective-permute-start.4) | collective-permute-done | bytes 229408 | tf_op jit(solution)/shard_map/ppermute | solution.py:253
  29.8 0.6 %chain.1 = (f32[4,8,256]{2,1,0:T(8,128)S(1)}, bf16[7,256,256]{2,1,0:T(8,128)(2,1)S(1)}) custom-call(f32[8,256]{1,0:T(8,128)S(1)} %get-tuple-element.36.refs_0_, bf16[4,7,16,256]{3,2,1,0:T(8,128)(2,1)S(1)} %fusion.5.refs_1_, bf16[4,7,16,256]{3,2,1,0:T(8,128)(2,1)S(1)} %collective-permute-done.4.refs_2_, ...), custom_call_target="tpu_custom_call" | custom-call | tf_op jit(solution)/shard_map/chain/pallas_call | solution.py:276
  30.4 0.0 collective-permute-start.7
  30.4 1.2 %collective-permute-done.7.o1 = f32[4,8,256]{2,1,0:T(8,128)S(1)} collective-permute-done((f32[4,8,256]{2,1,0:T(8,128)S(1)}, f32[4,8,256]{2,1,0:T(8,128)S(1)}, u32[]{:S(2)}, u32[]{:S(2)}) %collective-permute-start.7) | collective-permute-done | bytes 32800 | tf_op jit(solution)/shard_map/ppermute | solution.py:327
  31.6 0.0 collective-permute-start.8
  31.6 1.5 %collective-permute-start.10 = (f32[2,8,256]{2,1,0:T(8,128)S(1)}, f32[2,8,256]{2,1,0:T(8,128)S(1)}, u32[]{:S(2)}, u32[]{:S(2)}) collective-permute-start(f32[2,8,256]{2,1,0:T(8,128)S(1)} %slice.39), channel_id=1, source_target_pairs={{0,96},{16,112},{32,64},{48,80},{64,32},{80,48},{96,0},{112,16},{1... | collective-permute-start | bytes 49160 | tf_op jit(solution)/shard_map/ppermute | solution.py:327
  33.1 2.0 %collective-permute-start.9 = (f32[2,8,256]{2,1,0:T(8,128)S(1)}, f32[2,8,256]{2,1,0:T(8,128)S(1)}, u32[]{:S(2)}, u32[]{:S(2)}) collective-permute-start(f32[2,8,256]{2,1,0:T(8,128)S(1)} %slice.39), channel_id=1, source_target_pairs={{0,64},{16,80},{32,96},{48,112},{64,0},{80,16},{96,32},{112,48},{1... | collective-permute-start | bytes 49160 | tf_op jit(solution)/shard_map/ppermute | solution.py:327
  35.1 2.3 %near.3.nb = f32[4,8,256]{2,1,0:T(8,128)S(1)} custom-call(s32[16,8]{1,0:T(8,128)S(1)} %broadcast_subtract_fusion.refs_0_.slots, bf16[16,16,256]{2,1,0:T(8,128)(2,1)S(1)} %collective-permute-done.2.refs_1_.left, bf16[16,16,256]{2,1,0:T(8,128)(2,1)S(1)} %get-tuple-element.58.own.refs_2_, bf16[16,16,256]{2,1,0:T(8,128)(2,1)S(1)} %collective-permute-done.3.refs_3_.right, ...), custom_call_target="tpu_custom_call" | custom-call | tf_op jit(solution)/shard_map/near/pallas_call | solution.py:216
  37.4 0.0 collective-permute-done.10.q3
  37.4 0.4 collective-permute-done.9.q2
  37.7 0.0 collective-permute-done.8.q1
  37.7 4.0 %collective-permute-start.11 = (f32[1,8,256]{2,1,0:T(8,128)S(1)}, f32[1,8,256]{2,1,0:T(8,128)S(1)}, u32[]{:S(2)}, u32[]{:S(2)}) collective-permute-start(f32[1,8,256]{2,1,0:T(8,128)S(1)} %fusion.7), channel_id=1, source_target_pairs={{0,192},{16,208},{32,224},{48,240},{64,128},{80,144},{96,160},{112... | collective-permute-start | bytes 24584 | tf_op jit(solution)/shard_map/ppermute | solution.py:327
  41.7 3.2 %near_fetch.1 = (f32[3,8,256]{2,1,0:T(8,128)S(1)}, s32[1,4096]{1,0:T(1,128)S(1)}, bf16[16,256,256]{2,1,0:T(8,128)(2,1)S(1)}, bf16[30,256,256]{2,1,0:T(8,128)(2,1)S(1)}, bf16[16,256,256]{2,1,0:T(8,128)(2,1)S(1)}) custom-call(s32[16,8]{1,0:T(8,128)S(1)} %broadcast_subtract_fusion.refs_0_.slots, bf16[16,16,256]{2,1,0:T(8,128)(2,1)S(1)} %collective-permute-done.2.refs_1_.left, ...), custom_call_target="tpu_custom_call" | custom-call | tf_op jit(solution)/shard_map/near_fetch/pallas_call | solution.py:228
  45.0 0.0 collective-permute-done.11.o3
  45.0 3.5 %down.1 = f32[4,4096]{1,0:T(4,128)} custom-call(f32[4,8,256]{2,1,0:T(8,128)S(1)} %collective-permute-done.7.o1, f32[3,8,256]{2,1,0:T(8,128)S(1)} %collective-permute-done.8.q1, f32[2,8,256]{2,1,0:T(8,128)S(1)} %collective-permute-done.9.q2, f32[2,8,256]{2,1,0:T(8,128)S(1)} %collective-permute-done.10.q3, f32[1,8,256]{2,1,0:T(8,128)S(1)} %collective-permute-done.11.o3, ...), custom_call_target="tpu_custom_call" | custom-call | tf_op jit(solution)/shard_map/down/pallas_call | solution.py:315
  (12 shorter events, 0.1 us)
Async XLA Ops:
  0.0 6.0 %copy-start = (bf16[1,4,2,16,256]{4,3,2,1,0:T(8,128)(2,1)S(1)}, bf16[1,4,2,16,256]{4,3,2,1,0:T(8,128)(2,1)}, u32[]{:S(2)}) copy-start(bf16[1,4,2,16,256]{4,3,2,1,0:T(8,128)(2,1)} %param.13) | copy-start | bytes 196612
  0.0 6.0 %collective-permute-start = (bf16[8,16,256]{2,1,0:T(8,128)(2,1)}, bf16[8,16,256]{2,1,0:T(8,128)(2,1)S(1)}, u32[]{:S(2)}, u32[]{:S(2)}) collective-permute-start(bf16[8,16,256]{2,1,0:T(8,128)(2,1)} %bitcast.3), channel_id=1, source_target_pairs={{0,8},{1,9},{2,10},{3,11},{4,12},{5,13},{6,14},{7,15},{8,0},{9,1},... | collective-permute-start | bytes 196616 | tf_op jit(solution)/shard_map/ppermute | solution.py:253
  6.0 11.5 %collective-permute-start.1 = (bf16[2,8,16,256]{3,2,1,0:T(8,128)(2,1)S(1)}, bf16[2,8,16,256]{3,2,1,0:T(8,128)(2,1)S(1)}, u32[]{:S(2)}, u32[]{:S(2)}) collective-permute-start(bf16[2,8,16,256]{3,2,1,0:T(8,128)(2,1)S(1)} %pad_maximum_fusion.1), channel_id=1, source_target_pairs={{0,6},{1,7},{2,4},{3,5},{4,10},{5,11},{6,8},{7,9},{8,14},{9,15},{1... | collective-permute-start | bytes 393224 | tf_op jit(solution)/shard_map/ppermute | solution.py:253
  10.2 7.3 %collective-permute-start.3 = (bf16[16,16,256]{2,1,0:T(8,128)(2,1)S(1)}, bf16[16,16,256]{2,1,0:T(8,128)(2,1)S(1)}, u32[]{:S(2)}, u32[]{:S(2)}) collective-permute-start(bf16[16,16,256]{2,1,0:T(8,128)(2,1)S(1)} %get-tuple-element.58.own.refs_2_), channel_id=1, source_target_pairs={{0,240},{16,0},{32,16},{48,32},{64,48},{80,64},{96,80},{112,96},{1... | collective-permute-start | bytes 393224 | tf_op jit(solution)/shard_map/ppermute | solution.py:349
  15.0 5.6 %collective-permute-start.2 = (bf16[16,16,256]{2,1,0:T(8,128)(2,1)S(1)}, bf16[16,16,256]{2,1,0:T(8,128)(2,1)S(1)}, u32[]{:S(2)}, u32[]{:S(2)}) collective-permute-start(bf16[16,16,256]{2,1,0:T(8,128)(2,1)S(1)} %get-tuple-element.58.own.refs_2_), channel_id=1, source_target_pairs={{0,16},{16,32},{32,48},{48,64},{64,80},{80,96},{96,112},{112,128},... | collective-permute-start | bytes 393224 | tf_op jit(solution)/shard_map/ppermute | solution.py:348
  15.0 8.5 %copy-start.1 = (s32[16,8]{0,1:T(8,128)S(1)}, s32[16,8]{0,1:T(8,128)}, u32[]{:S(2)}) copy-start(s32[16,8]{0,1:T(8,128)} %param.10) | copy-start | bytes 1540
  20.7 7.8 %collective-permute-start.6 = (bf16[4,7,16,256]{3,2,1,0:T(8,128)(2,1)S(1)}, bf16[4,7,16,256]{3,2,1,0:T(8,128)(2,1)S(1)}, u32[]{:S(2)}, u32[]{:S(2)}) collective-permute-start(bf16[4,7,16,256]{3,2,1,0:T(8,128)(2,1)S(1)} %fusion.5.refs_1_), channel_id=1, source_target_pairs={{0,4},{1,5},{2,6},{3,7},{4,8},{5,9},{6,10},{7,11},{8,12},{9,13},{1... | collective-permute-start | bytes 688136 | tf_op jit(solution)/shard_map/ppermute | solution.py:253
  21.4 7.1 %collective-permute-start.5 = (bf16[4,7,16,256]{3,2,1,0:T(8,128)(2,1)S(1)}, bf16[4,7,16,256]{3,2,1,0:T(8,128)(2,1)S(1)}, u32[]{:S(2)}, u32[]{:S(2)}) collective-permute-start(bf16[4,7,16,256]{3,2,1,0:T(8,128)(2,1)S(1)} %fusion.5.refs_1_), channel_id=1, source_target_pairs={{0,3},{1,0},{2,1},{3,2},{4,7},{5,4},{6,5},{7,6},{8,11},{9,8},{10,9... | collective-permute-start | bytes 688136 | tf_op jit(solution)/shard_map/ppermute | solution.py:253
  22.5 7.2 %collective-permute-start.4 = (bf16[4,7,16,256]{3,2,1,0:T(8,128)(2,1)S(1)}, bf16[4,7,16,256]{3,2,1,0:T(8,128)(2,1)S(1)}, u32[]{:S(2)}, u32[]{:S(2)}) collective-permute-start(bf16[4,7,16,256]{3,2,1,0:T(8,128)(2,1)S(1)} %fusion.5.refs_1_), channel_id=1, source_target_pairs={{0,1},{1,2},{2,3},{3,0},{4,5},{5,6},{6,7},{7,4},{8,9},{9,10},{10,1... | collective-permute-start | bytes 688136 | tf_op jit(solution)/shard_map/ppermute | solution.py:253
  30.4 1.2 %collective-permute-start.7 = (f32[4,8,256]{2,1,0:T(8,128)S(1)}, f32[4,8,256]{2,1,0:T(8,128)S(1)}, u32[]{:S(2)}, u32[]{:S(2)}) collective-permute-start(f32[4,8,256]{2,1,0:T(8,128)S(1)} %get-tuple-element.51), channel_id=1, source_target_pairs={{0,16},{16,0},{32,48},{48,32},{64,80},{80,64},{96,112},{112,96},{1... | collective-permute-start | bytes 98312 | tf_op jit(solution)/shard_map/ppermute | solution.py:327
  31.6 6.2 %collective-permute-start.8 = (f32[3,8,256]{2,1,0:T(8,128)S(1)}, f32[3,8,256]{2,1,0:T(8,128)S(1)}, u32[]{:S(2)}, u32[]{:S(2)}) collective-permute-start(f32[3,8,256]{2,1,0:T(8,128)S(1)} %slice_add_fusion), channel_id=1, source_target_pairs={{0,32},{16,48},{32,0},{48,16},{64,96},{80,112},{96,64},{112,80},{1... | collective-permute-start | bytes 73736 | tf_op jit(solution)/shard_map/ppermute | solution.py:327
  31.6 5.8 %collective-permute-start.10 = (f32[2,8,256]{2,1,0:T(8,128)S(1)}, f32[2,8,256]{2,1,0:T(8,128)S(1)}, u32[]{:S(2)}, u32[]{:S(2)}) collective-permute-start(f32[2,8,256]{2,1,0:T(8,128)S(1)} %slice.39), channel_id=1, source_target_pairs={{0,96},{16,112},{32,64},{48,80},{64,32},{80,48},{96,0},{112,16},{1... | collective-permute-start | bytes 49160 | tf_op jit(solution)/shard_map/ppermute | solution.py:327
  33.1 4.6 %collective-permute-start.9 = (f32[2,8,256]{2,1,0:T(8,128)S(1)}, f32[2,8,256]{2,1,0:T(8,128)S(1)}, u32[]{:S(2)}, u32[]{:S(2)}) collective-permute-start(f32[2,8,256]{2,1,0:T(8,128)S(1)} %slice.39), channel_id=1, source_target_pairs={{0,64},{16,80},{32,96},{48,112},{64,0},{80,16},{96,32},{112,48},{1... | collective-permute-start | bytes 49160 | tf_op jit(solution)/shard_map/ppermute | solution.py:327
  37.7 7.2 %collective-permute-start.11 = (f32[1,8,256]{2,1,0:T(8,128)S(1)}, f32[1,8,256]{2,1,0:T(8,128)S(1)}, u32[]{:S(2)}, u32[]{:S(2)}) collective-permute-start(f32[1,8,256]{2,1,0:T(8,128)S(1)} %fusion.7), channel_id=1, source_target_pairs={{0,192},{16,208},{32,224},{48,240},{64,128},{80,144},{96,160},{112... | collective-permute-start | bytes 24584 | tf_op jit(solution)/shard_map/ppermute | solution.py:327
